TPU v7x, 128 devices: a whole 4x4x4 slice. The times are simulated.
128 devices in a mesh: vocab: 32 (over x, y, core), rows: 4 (over z).
Axes of the slice: x: 4, y: 4, z: 4, core: 2. Of those that a mesh axis runs over, the one named last changes fastest.
Arguments:
- hidden_states: bfloat16 [2048, 5120], P('rows', 'vocab'), may hold values from -104 to 104
- head_weight: bfloat16 [5120, 151936], P(None, ('vocab', 'rows')), may hold values from -0.078125 to 0.078125
- sign_bits: int32 [151936], P(('vocab', 'rows')), may hold values from 0 to 1
- bucket_ids: int32 [151936], P(('vocab', 'rows')), may hold values from 0 to 511
Outputs:
- sketch: float32 [2048, 512], P('rows', 'vocab')
- peak_logprob: float32 [2048], P('rows')
All inputs are finite; a program needn't handle non-finite values.
Results may differ from a plain program's by a relative error of at most 0.0025.
Values may be sent and summed in bfloat16 or wider, within the bound.
No kernel may reach another device: no remote copies, remote signals or barrier semaphores. Data moves between devices by JAX's collectives and lax.ppermute only.
A program may use at most 128 MiB of HBM per device.

v0:
```python
import jax
import jax.numpy as jnp
from jax import lax
from jax.sharding import PartitionSpec as P

V = 151936
B = 512


def per_device(hidden_states, head_weight, sign_bits, bucket_ids):
    columns = head_weight.shape[1]
    group_rows = hidden_states.shape[0]
    gathered_rows = lax.all_gather(hidden_states, "rows", axis=0, tiled=True)
    logits = jnp.dot(
        lax.all_gather(gathered_rows, "vocab", axis=1, tiled=True),
        head_weight,
        preferred_element_type=jnp.float32,
    )
    signs = (2 * sign_bits - 1).astype(jnp.float32)
    buckets = lax.broadcasted_iota(jnp.int32, (columns, B), 1)
    sign_table = jnp.where(bucket_ids[:, None] == buckets, signs[:, None], jnp.float32(0.0)).astype(
        jnp.bfloat16
    )
    factor = jnp.sqrt(jnp.float32(V) * jnp.float32(B))
    offset_rows = lax.axis_index("rows") * group_rows
    row_max = lax.pmax(jnp.max(logits, axis=1), ("vocab", "rows"))
    exponent = jnp.exp(logits - row_max[:, None])
    row_total = lax.psum(jnp.sum(exponent, axis=1), ("vocab", "rows"))
    exponent_bf = exponent.astype(jnp.bfloat16)
    partial_value = jnp.dot(exponent_bf, sign_table, preferred_element_type=jnp.float32)
    bucket_part = lax.psum_scatter(partial_value, "vocab", scatter_dimension=1, tiled=True)
    owned_share = lax.psum_scatter(bucket_part, "rows", scatter_dimension=0, tiled=True)
    owned_total = lax.dynamic_slice_in_dim(row_total, offset_rows, group_rows, 0)
    sketch = owned_share / owned_total[:, None] * factor
    peak_logprob = -jnp.log(owned_total)
    return (sketch, peak_logprob)


def solution(mesh):
    return jax.shard_map(
        per_device,
        mesh=mesh,
        in_specs=(
            P("rows", "vocab"),
            P(None, ("vocab", "rows")),
            P(("vocab", "rows")),
            P(("vocab", "rows")),
        ),
        out_specs=(P("rows", "vocab"), P("rows")),
        check_vma=False,
    )
```

profile of v0, /device:TPU:0, one launch (start us, length us, event | category | flops | bytes accessed | tf_op | source)
XLA Modules:
  0.0 371.1 jit_solution(2686845280562800768)
XLA Ops:
  7.2 0.0 all-gather.2.cloned.1.call-start
  7.2 16.6 %all_gather.6 = bf16[2048,160]{0,1:T(8,128)(2,1)} all-gather(bf16[512,160]{0,1:T(8,128)(2,1)} %param.4), channel_id=1, replica_groups=mesh['vocab'=32,'rows'=4] {'rows'}, dimensions={0}, use_global_device_ids=true | all-gather | bytes 819200 | tf_op jit(solution)/shard_map/all_gather | solution.py:13
  23.8 0.0 all-gather.2.cloned.1.call-update
  23.8 0.0 reduce-scatter.3.cloned.1.call-start
  23.9 0.7 add_convert_fusion
  24.6 0.0 copy-start
  24.6 81.4 %all-gather.2.cloned.1.call-done = bf16[2048,5120]{0,1:T(8,128)(2,1)} async-done(((bf16[2048,160]{0,1:T(8,128)(2,1)}), bf16[2048,5120]{0,1:T(8,128)(2,1)}) %all-gather.2.cloned.1.call-update) | async-done | bytes 20971536 | tf_op jit(solution)/shard_map/all_gather | solution.py:15
  106.0 33.5 %fusion.9 = (f32[2048]{0:T(1024)S(1)}, f32[2048,1187]{0,1:T(8,128)}) fusion(bf16[2048,5120]{0,1:T(8,128)(2,1)} %all-gather.2.cloned.1.call-done, bf16[5120,1187]{0,1:T(8,128)(2,1)} %param.5), kind=kOutput, calls=%fused_computation.14 | convolution fusion | flops 24895623168 | bytes 42858496 | tf_op jit(solution)/shard_map/dot_general | solution.py:14
  139.5 65.0 %pmax.7 = f32[2048]{0:T(1024)S(1)} all-reduce(f32[2048]{0:T(1024)S(1)} %get-tuple-element.4), channel_id=1, replica_groups=mesh['vocab'=32,'rows'=4] {'vocab','rows'}, use_global_device_ids=true, to_apply=%region_1.2 | all-reduce | flops 2048 | bytes 16384 | tf_op jit(solution)/shard_map/pmax | solution.py:26
  204.5 0.0 copy-done
  204.5 8.8 %fusion.2 = f32[2048,512]{0,1:T(8,128)} fusion(f32[2048,1187]{0,1:T(8,128)} %get-tuple-element.5, f32[2048]{0:T(1024)S(1)} %pmax.7, bf16[1187]{0:T(1024)(128)(2,1)S(1)} %add_convert_fusion, s32[1187]{0:T(1024)S(1)} %copy-done), kind=kOutput, calls=%fused_computation.3 | convolution fusion | flops 2495396864 | bytes 13933522 | tf_op jit(solution)/shard_map/dot_general | solution.py:30
  213.3 0.0 reduce-scatter.3.cloned.1.call-update
  213.3 0.0 reduce-scatter.5.cloned.1.call-start
  213.4 79.1 %reduce-scatter.3.cloned.1.call-done = f32[2048,16]{0,1:T(8,128)} async-done(((f32[2048,512]{0,1:T(8,128)}), f32[2048,16]{0,1:T(8,128)}) %reduce-scatter.3.cloned.1.call-update) | async-done | bytes 131088 | tf_op jit(solution)/shard_map/reduce_scatter | solution.py:31
  292.5 0.0 reduce-scatter.5.cloned.1.call-update
  292.5 5.1 %fusion = f32[2048]{0:T(1024)S(1)} fusion(f32[2048,1187]{0,1:T(8,128)} %get-tuple-element.5, f32[2048]{0:T(1024)S(1)} %pmax.7), kind=kLoop, calls=%fused_computation.1 | loop fusion | flops 4859904 | bytes 9740288 | tf_op jit(solution)/shard_map/reduce_sum | solution.py:28
  297.6 64.9 %psum.7 = f32[2048]{0:T(1024)S(1)} all-reduce(f32[2048]{0:T(1024)S(1)} %fusion), channel_id=1, replica_groups=mesh['vocab'=32,'rows'=4] {'vocab','rows'}, use_global_device_ids=true, to_apply=%region_5.6 | all-reduce | flops 2048 | bytes 16384 | tf_op jit(solution)/shard_map/psum | solution.py:28
  362.5 0.7 log_negate_fusion
  363.2 0.0 reduce-scatter.5.cloned.1.call-done
  363.2 1.4 divide_multiply_fusion
Async XLA Ops:
  7.2 98.9 %all-gather.2.cloned.1.call-start = ((), (), s32[]{:S(2)}) async-start(), calls=%async_computation.2 | async-start | bytes 21626880 | tf_op jit(solution)/shard_map/all_gather | solution.py:15
  23.8 268.6 %reduce-scatter.3.cloned.1.call-start = ((), (), s32[]{:S(2)}) async-start(), calls=%async_computation.3 | async-start | bytes 4325376 | tf_op jit(solution)/shard_map/reduce_scatter | solution.py:31
  24.6 179.9 %copy-start = (s32[1187]{0:T(1024)S(1)}, s32[1187]{0:T(1024)}, u32[]{:S(2)}) copy-start(s32[1187]{0:T(1024)} %param.7) | copy-start | bytes 14248
  213.3 149.9 %reduce-scatter.5.cloned.1.call-start = ((), (), s32[]{:S(2)}) async-start(), calls=%async_computation.4 | async-start | bytes 163840 | tf_op jit(solution)/shard_map/reduce_scatter | solution.py:32
Sparse Core Ops, SparseCore 0:
  24.0 82.0 all-gather.1
  213.4 78.9 reduce-scatter.2
  294.9 20.0 reduce-scatter.4
where the time goes:
time: 372 us; the launch traced here: 371 us
  waiting for transfers between devices  161 us (43%)
  blocking collectives  147 us (40%)
  matrix products  42.2 us (11%)
  between operations  13.8 us (4%)
  other arithmetic  7.88 us (2%)
    all_gather x1, waiting for transfers between devices, per_device(): lax.all_gather(gathered_rows, 'vocab', axis=1, tiled=True)  81.4 us
    reduce_scatter x1, waiting for transfers between devices, per_device(): lax.psum_scatter(partial_value, 'vocab', scatter_dimension=1, tiled=True)  79.1 us
    pmax x1, blocking collectives, per_device(): row_max = lax.pmax(jnp.max(logits, axis=1), ('vocab', 'rows'))  65 us
    psum x1, blocking collectives, per_device(): row_total = lax.psum(jnp.sum(exponent, axis=1), ('vocab', 'rows'))  64.9 us
    dot_general x1, matrix products, per_device(): jnp.dot(lax.all_gather(gathered_rows, 'vocab', axis=1, tiled=True), head_...  33.5 us
    all_gather x1, blocking collectives, per_device(): gathered_rows = lax.all_gather(hidden_states, 'rows', axis=0, tiled=True)  16.6 us
    dot_general x1, matrix products, per_device(): jnp.dot(exponent_bf, sign_table, preferred_element_type=jnp.float32)  8.78 us
  transfers between devices with their start and end apart: 3, of which 2 were waited for; matrix products, arithmetic and copies ran while one was open for 2% of the time, Pallas kernels for 0%

commit v1 on v0

v1 whole, which is shorter than its diff:
```python
import functools

import jax
import jax.numpy as jnp
from jax import lax
from jax.experimental import pallas as pl
from jax.experimental.pallas import tpu as pltpu
from jax.sharding import PartitionSpec as P

V = 151936
B = 512
LANES = 128


def split_bf16(value):
    high = value.astype(jnp.bfloat16).astype(jnp.float32)
    low = (value - high).astype(jnp.bfloat16).astype(jnp.float32)
    return high, low


def sketch_kernel(w_ref, x_ref, ids_ref, sign_ref, out_ref, table_ref, *, groups, owners):
    columns = w_ref.shape[0]
    own = B // owners

    @pl.when(pl.program_id(0) == 0)
    def _():
        buckets = lax.broadcasted_iota(jnp.int32, (B, columns), 0)
        signs = (2 * sign_ref[...] - 1).astype(jnp.float32)
        table_ref[...] = jnp.where(buckets == ids_ref[...], signs, 0.0).astype(jnp.bfloat16)

    logits = jnp.dot(w_ref[...], x_ref[0], preferred_element_type=jnp.float32)
    max_high, max_low = split_bf16(jnp.max(logits, axis=0, keepdims=True))
    exponent = jnp.exp(logits - (max_high + max_low))
    total_high, total_low = split_bf16(jnp.sum(exponent, axis=0, keepdims=True))
    sums = jnp.dot(table_ref[...], exponent.astype(jnp.bfloat16), preferred_element_type=jnp.float32)
    for g in range(groups):
        lanes = slice(LANES * g, LANES * g + LANES)
        out_ref[:, 0, own * g : own * g + own, :] = sums[:, lanes].reshape(owners, own, LANES)
    rows = [kind[:, LANES * g : LANES * g + LANES] for kind in (max_high, max_low, total_high, total_low) for g in range(groups)]
    stats = jnp.concatenate(rows, axis=0)
    out_ref[:, 0, own * groups :, :] = jnp.broadcast_to(stats[None], (owners,) + stats.shape)


def partial_sums(weights, tokens, bucket_ids, sign_bits, owners):
    columns, depth = weights.shape
    blocks, _, width = tokens.shape
    groups = width // LANES
    rows = (B // owners + 4) * groups
    return pl.pallas_call(
        functools.partial(sketch_kernel, groups=groups, owners=owners),
        grid=(blocks,),
        in_specs=[
            pl.BlockSpec((columns, depth), lambda i: (0, 0), pipeline_mode=pl.Buffered(1)),
            pl.BlockSpec((1, depth, width), lambda i: (i, 0, 0)),
            pl.BlockSpec((1, columns), lambda i: (0, 0)),
            pl.BlockSpec((1, columns), lambda i: (0, 0)),
        ],
        out_specs=pl.BlockSpec((owners, 1, rows, LANES), lambda i: (0, i, 0, 0)),
        out_shape=jax.ShapeDtypeStruct((owners, blocks, rows, LANES), jnp.float32),
        scratch_shapes=[pltpu.VMEM((B, columns), jnp.bfloat16)],
        compiler_params=pltpu.CompilerParams(vmem_limit_bytes=56 * 2**20),
        cost_estimate=pl.CostEstimate(
            flops=2 * columns * (depth + B) * blocks * width,
            bytes_accessed=2 * depth * (columns + blocks * width),
            transcendentals=columns * blocks * width,
        ),
    )(weights, tokens, bucket_ids[None, :], sign_bits[None, :])


def per_device(hidden_states, head_weight, sign_bits, bucket_ids):
    owners = lax.axis_size("vocab")
    blocks = lax.axis_size("rows")
    width = hidden_states.shape[0]
    groups = width // LANES
    own = B // owners
    tokens = lax.all_gather(hidden_states.T, ("rows", "vocab"), axis=0, tiled=True)
    tokens = tokens.reshape(blocks, owners * hidden_states.shape[1], width)
    parts = partial_sums(head_weight.T, tokens, bucket_ids, sign_bits, owners)
    sent = parts.astype(jnp.float16).reshape(owners * blocks, parts.shape[2], LANES)
    received = lax.all_to_all(sent, ("vocab", "rows"), 0, 0, tiled=True).astype(jnp.float32)
    sums = received[:, : own * groups].reshape(-1, groups, own, LANES)
    stats = received[:, own * groups :].reshape(-1, 4, groups, LANES)
    local_max = stats[:, 0] + stats[:, 1]
    row_max = jnp.max(local_max, axis=0)
    rescale = jnp.exp(local_max - row_max)
    row_total = jnp.sum((stats[:, 2] + stats[:, 3]) * rescale, axis=0)
    bucket_sums = jnp.sum(sums * rescale[:, :, None, :], axis=0)
    factor = jnp.sqrt(jnp.float32(V) * jnp.float32(B))
    sketch = bucket_sums / row_total[:, None, :] * factor
    return (sketch.transpose(0, 2, 1).reshape(width, own), -jnp.log(row_total).reshape(width))


def solution(mesh):
    return jax.shard_map(
        per_device,
        mesh=mesh,
        in_specs=(
            P("rows", "vocab"),
            P(None, ("vocab", "rows")),
            P(("vocab", "rows")),
            P(("vocab", "rows")),
        ),
        out_specs=(P("rows", "vocab"), P("rows")),
        check_vma=False,
    )
```

time: 372 us -> 196 us (0.53)
  blocking collectives: 147 us -> 43.7 us
  waiting for transfers between devices: 161 us -> 90.8 us
  matrix products: 42.2 us -> 0 us
  Pallas kernels: 0 us -> 38.1 us
    reduce_scatter x2 -> x0, waiting for transfers between devices: 79.1 us -> none  [the longest x1 79.1 us: per_device(): lax.psum_scatter(partial_value, 'vocab', scatter_dimension=1, tiled=True)]
    pmax x1 -> x0, blocking collectives: 65 us -> none  [per_device(): row_max = lax.pmax(jnp.max(logits, axis=1), ('vocab', 'rows'))]
    psum x1 -> x0, blocking collectives: 64.9 us -> none  [per_device(): row_total = lax.psum(jnp.sum(exponent, axis=1), ('vocab', 'rows'))]
    all_to_all x0 -> x1, blocking collectives: none -> 43.7 us  [per_device(): lax.all_to_all(sent, ('vocab', 'rows'), 0, 0, tiled=True)]
    dot_general x2 -> x0, matrix products: 42.2 us -> none  [the longest x1 33.5 us: per_device(): jnp.dot(lax.all_gather(gathered_rows, 'vocab', axis=1, tiled=True), head_...]
    pallas_call x0 -> x1, Pallas kernels: none -> 38.1 us  [partial_sums(): pl.pallas_call(functools.partial(sketch_kernel, groups=groups, owners=own...]
    all_gather x1 -> x0, blocking collectives: 16.6 us -> none  [per_device(): gathered_rows = lax.all_gather(hidden_states, 'rows', axis=0, tiled=True)]
    all_gather x1, waiting for transfers between devices: 81.4 us -> 90.2 us  [per_device(): lax.all_gather(hidden_states.T, ('rows', 'vocab'), axis=0, tiled=True)]
  transfers between devices with their start and end apart: 3 -> 1, of which waited for: 2 -> 1; matrix products, arithmetic and copies ran while one was open for 2% -> 1% of each run, Pallas kernels for 0% -> 0%
where the time goes in v1:
time: 196 us; the launch traced here: 195 us
  waiting for transfers between devices  90.8 us (46%)
  blocking collectives  43.7 us (22%)
  Pallas kernels  38.1 us (19%)
  between operations  14.1 us (7%)
  other arithmetic  5.56 us (3%)
  local copies, waits for them, and re-layouts  2.65 us (1%)
    all_gather x1, waiting for transfers between devices, per_device(): lax.all_gather(hidden_states.T, ('rows', 'vocab'), axis=0, tiled=True)  90.2 us
    all_to_all x1, blocking collectives, per_device(): lax.all_to_all(sent, ('vocab', 'rows'), 0, 0, tiled=True)  43.7 us
    pallas_call x1, Pallas kernels, partial_sums(): pl.pallas_call(functools.partial(sketch_kernel, groups=groups, owners=own...  38.1 us
  transfers between devices with their start and end apart: 1, of which 1 were waited for; matrix products, arithmetic and copies ran while one was open for 1% of the time, Pallas kernels for 0%

profile of v1, /device:TPU:0, one launch (start us, length us, event | category | flops | bytes accessed | tf_op | source)
XLA Modules:
  0.0 195.0 jit_solution(6325073009064558729)
XLA Ops:
  7.2 0.0 all-gather.2.cloned.1.call-start
  7.2 0.7 all-gather.2.cloned.1.call-update
  7.9 1.3 broadcast_in_dim.10.sign_ref
  9.2 1.3 broadcast_in_dim.4.ids_ref
  10.5 90.2 %all-gather.2.cloned.1.call-done = bf16[20480,512]{1,0:T(8,128)(2,1)} async-done(((bf16[160,512]{1,0:T(8,128)(2,1)}), bf16[20480,512]{1,0:T(8,128)(2,1)}) %all-gather.2.cloned.1.call-update) | async-done | bytes 20971536 | tf_op jit(solution)/shard_map/all_gather | solution.py:76
  100.6 38.1 %shard_map.59 = f32[32,4,80,128]{3,2,1,0:T(8,128)} custom-call(bf16[1187,5120]{1,0:T(8,128)(2,1)} %bitcast.51, bf16[4,5120,512]{2,1,0:T(8,128)(2,1)} %bitcast.50, s32[1,1187]{1,0:T(1,128)} %broadcast_in_dim.4.ids_ref, s32[1,1187]{1,0:T(1,128)} %broadcast_in_dim.10.sign_ref), custom_call_target="tpu_custom_call" | custom-call | flops 27382513664 | bytes 33126400 | tf_op jit(solution)/shard_map/pallas_call | solution.py:49
  138.7 3.0 %convert_element_type.6 = f16[32,4,80,128]{3,2,1,0:T(8,128)(2,1)S(1)} convert(f32[32,4,80,128]{3,2,1,0:T(8,128)} %shard_map.59) | non-fusion elementwise | flops 1310720 | bytes 7864320 | tf_op jit(solution)/shard_map/convert_element_type | solution.py:79
  141.7 43.7 %all_to_all.5 = f16[128,80,128]{2,1,0:T(8,128)(2,1)S(1)} all-to-all(f16[128,80,128]{2,1,0:T(8,128)(2,1)S(1)} %bitcast.45), channel_id=1, replica_groups=mesh['vocab'=32,'rows'=4] {'vocab','rows'}, dimensions={0} | all-to-all | bytes 5242880 | tf_op jit(solution)/shard_map/all_to_all | solution.py:80
  185.4 0.4 convert_element_type.7
  185.8 0.1 slice.25
  185.9 0.1 fusion.6
  186.1 0.2 fusion.3
  186.2 0.7 fusion
  186.9 0.6 negate_bitcast_fusion
  187.5 0.6 copy_bitcast_fusion
Async XLA Ops:
  7.2 93.5 %all-gather.2.cloned.1.call-start = ((), (), s32[]{:S(2)}) async-start(), calls=%async_computation.1 | async-start | bytes 21135360 | tf_op jit(solution)/shard_map/all_gather | solution.py:76
Sparse Core Ops, SparseCore 0:
  11.0 89.6 all-gather.1

commit v2 on v0

v2 whole, which is shorter than its diff:
```python
import functools

import jax
import jax.numpy as jnp
from jax import lax
from jax.experimental import pallas as pl
from jax.experimental.pallas import tpu as pltpu
from jax.sharding import PartitionSpec as P

V = 151936
B = 512
LANES = 128
SIDE = 4
CORES = 2
PLANE = SIDE * SIDE
DEVICES = SIDE * PLANE * CORES
OWN = B // (PLANE * CORES)
KINDS = 4
BOTH = ("vocab", "rows")
X, Y, Z = 0, 1, 2
ROW_BLOCK = 304
VMEM_BYTES = 44 * 2**20
PLACE_BYTES = 32 * 2**20
ANY = pl.BlockSpec(memory_space=pl.ANY)


def coordinates(device):
    vocab, z = divmod(device, SIDE)
    chip, core = divmod(vocab, CORES)
    return chip // SIDE, chip % SIDE, z, core


def device_at(x, y, z, core):
    return ((x * SIDE + y) * CORES + core) * SIDE + z


def permute(array, target):
    pairs = [(i, device_at(*target(*coordinates(i)))) for i in range(DEVICES)]
    return lax.ppermute(array, BOTH, pairs)


def shift(array, axis, step):
    def target(x, y, z, core):
        place = [x, y, z]
        place[axis] = (place[axis] + step) % SIDE
        return (*place, core)

    return permute(array, target)


def ring(array, axis):
    def target(x, y, z, core):
        place = [x, y, z]
        place[axis] = (place[axis] + (1 if core == 0 else -1)) % SIDE
        return (*place, core)

    return permute(array, target)


def swap(array):
    return permute(array, lambda x, y, z, core: (x, y, z, 1 - core))


def position():
    vocab = lax.axis_index("vocab")
    chip = vocab // CORES
    return (chip // SIDE, chip % SIDE, lax.axis_index("rows")), vocab % CORES


def place_first_kernel(own, lower, upper, far, out_a, out_b, sem):
    coords, _ = position()
    half = out_a.shape[2]
    copies = []
    for k, (piece, step) in enumerate(((own, 0), (lower, -1), (upper, 1), (far, 2))):
        slot = lax.rem(coords[Y] + SIDE + step, SIDE)
        copies.append(pltpu.make_async_copy(piece.at[:, pl.ds(0, half)], out_a.at[slot], sem.at[2 * k]))
        copies.append(pltpu.make_async_copy(piece.at[:, pl.ds(half, half)], out_b.at[slot], sem.at[2 * k + 1]))
    for copy in copies:
        copy.start()
    for copy in copies:
        copy.wait()


def place_second_kernel(*refs):
    coords, _ = position()
    outs, sem = refs[8:10], refs[10]
    copies = []
    for part, axis in enumerate((X, Z)):
        for k, step in enumerate((0, -1, 1, 2)):
            slot = lax.rem(coords[axis] + SIDE + step, SIDE)
            copies.append(pltpu.make_async_copy(refs[4 * part + k], outs[part].at[slot], sem.at[4 * part + k]))
    for copy in copies:
        copy.start()
    for copy in copies:
        copy.wait()


def place(kernel, pieces, shape):
    return pl.pallas_call(
        kernel,
        out_shape=[jax.ShapeDtypeStruct(shape, pieces[0].dtype)] * 2,
        out_specs=[ANY] * 2,
        scratch_shapes=[pltpu.SemaphoreType.DMA((8,))],
        compiler_params=pltpu.CompilerParams(vmem_limit_bytes=PLACE_BYTES),
    )(*pieces)


def around(array, axis):
    return (array, shift(array, axis, 1), shift(array, axis, -1), shift(array, axis, 2))


def split_bf16(value):
    high = value.astype(jnp.bfloat16).astype(jnp.float32)
    low = (value - high).astype(jnp.bfloat16).astype(jnp.float32)
    return high, low


def summarise(logits, table, core, store):
    max_high, max_low = split_bf16(jnp.max(logits, axis=0, keepdims=True))
    exponent = jnp.exp(logits - (max_high + max_low))
    total_high, total_low = split_bf16(jnp.sum(exponent, axis=0, keepdims=True))
    sums = jnp.dot(table, exponent.astype(jnp.bfloat16), preferred_element_type=jnp.float32)
    groups = logits.shape[1] // LANES
    pieces = [sums[:, LANES * g : LANES * g + LANES].reshape(PLANE, CORES, OWN, LANES) for g in range(groups)]
    kinds = (max_high, max_low, total_high, total_low)
    stats = [[kind[:, LANES * g : LANES * g + LANES] for g in range(groups)] for kind in kinds]
    store(pieces, stats)


def write(piece_refs, pieces, stats, core):
    kept_ref, sent_ref = piece_refs
    for g, piece in enumerate(pieces):
        rows = slice(OWN * g, OWN * g + OWN)
        kept_ref[:, rows, :] = jnp.where(core == 0, piece[:, 0], piece[:, 1])
        sent_ref[:, rows, :] = jnp.where(core == 0, piece[:, 1], piece[:, 0])
    rows = jnp.concatenate([row for kind in stats for row in kind], axis=0)
    rows = jnp.broadcast_to(rows[None], (PLANE,) + rows.shape)
    kept_ref[:, OWN * len(pieces) :, :] = rows
    sent_ref[:, OWN * len(pieces) :, :] = rows


def whole_kernel(w_ref, table_ref, *refs, which):
    count = len(which)
    buffers, refs = refs[: 2 * count], refs[2 * count :]
    kept_out, sent_out, held, logits, kept, sent, sem = refs[-7:]
    step = pl.program_id(0)
    (_, _, z), core = position()
    columns, depth = table_ref.shape[1], w_ref.shape[1]
    half = held.shape[4] // count

    def loads():
        for b in range(count):
            lanes = pl.ds(half * b, half)
            for k in range(2):
                same = (which[b] != "back") == (k == 0)
                c = core if same else 1 - core
                yield pltpu.make_async_copy(buffers[2 * b + k], held.at[:, :, c, :, lanes], sem.at[2 * b + k])

    @pl.when(step == 0)
    def _():
        copies = list(loads())
        for copy in copies:
            copy.start()
        for copy in copies:
            copy.wait()

    tokens = held[...].reshape(depth, half * count)
    logits[pl.ds(pl.multiple_of(step * ROW_BLOCK, ROW_BLOCK), ROW_BLOCK), :] = jnp.dot(
        w_ref[...], tokens, preferred_element_type=jnp.float32
    )

    @pl.when(step == pl.num_programs(0) - 1)
    def _():
        direction = 2 * core - 1
        groups = half // LANES

        def store(pieces, stats):
            copies = []
            for b in range(count):
                part = slice(groups * b, groups * b + groups)
                write((kept.at[b], sent.at[b]), pieces[part], [kind[part] for kind in stats], core)
                move = {"own": 0, "near": direction, "back": -direction, "far": 2}[which[b]]
                block = lax.rem(z + SIDE + move, SIDE)
                copies.append(pltpu.make_async_copy(kept.at[b], kept_out.at[:, block], sem.at[2 * b]))
                copies.append(pltpu.make_async_copy(sent.at[b], sent_out.at[:, block], sem.at[2 * b + 1]))
            for copy in copies:
                copy.start()
            for copy in copies:
                copy.wait()

        summarise(logits[:columns, :], table_ref[...], core, store)


def message_rows(half):
    return (OWN + KINDS) * (half // LANES)


def whole_blocks(weights, table, which, buffers, previous):
    columns, depth = weights.shape
    features, half = buffers[0].shape[2:]
    count = len(which)
    width = half * count
    rows = message_rows(half)
    steps = pl.cdiv(columns, ROW_BLOCK)
    shape = jax.ShapeDtypeStruct((PLANE, SIDE, rows, LANES), jnp.float32)
    return pl.pallas_call(
        functools.partial(whole_kernel, which=which),
        grid=(steps,),
        in_specs=[pl.BlockSpec((ROW_BLOCK, depth), lambda i: (i, 0)), pl.BlockSpec(table.shape, lambda i: (0, 0))]
        + [ANY] * (2 * count + len(previous)),
        out_specs=[ANY, ANY],
        out_shape=[shape, shape],
        input_output_aliases={2 + 2 * count + k: k for k in range(len(previous))},
        scratch_shapes=[
            pltpu.VMEM((SIDE, SIDE, CORES, features, width), jnp.bfloat16),
            pltpu.VMEM((steps * ROW_BLOCK, width), jnp.float32),
            pltpu.VMEM((count, PLANE, rows, LANES), jnp.float32),
            pltpu.VMEM((count, PLANE, rows, LANES), jnp.float32),
            pltpu.SemaphoreType.DMA((2 * count,)),
        ],
        compiler_params=pltpu.CompilerParams(vmem_limit_bytes=VMEM_BYTES),
        cost_estimate=pl.CostEstimate(
            flops=2 * columns * (depth + B) * width,
            bytes_accessed=2 * depth * (columns + width),
            transcendentals=columns * width,
        ),
    )(weights, table, *buffers, *previous)


def finish_kernel(w_hbm, table_ref, *refs):
    far_a, part_b, refs = refs[:2], refs[2:10], refs[12:]
    outs_a, outs_b, refs = refs[:2], refs[2:4], refs[4:]
    weights, held, logits, kept, sent, w_sem, x_sem, out_sem = refs
    step = pl.program_id(0)
    (x, _, z), core = position()
    columns = table_ref.shape[1]
    half = held.shape[5] // 2
    groups = half // LANES
    depth = weights.shape[1]
    direction = 2 * core - 1

    def w_copy(k):
        rows = pl.ds(ROW_BLOCK * k, min(ROW_BLOCK, columns - ROW_BLOCK * k))
        return pltpu.make_async_copy(w_hbm.at[rows], weights.at[rows], w_sem.at[k])

    def fetch_b(pair, slot):
        for k in range(8):
            move = (0, 0, direction, direction, -direction, -direction, 2, 2)[k]
            c = core if k in (0, 2, 5, 6) else 1 - core
            for h in range(2):
                target = held.at[slot, lax.rem(x + SIDE + move, SIDE), :, c, :, pl.ds(half * h, half)]
                pltpu.make_async_copy(part_b[k].at[2 * pair + h], target, x_sem.at[slot]).start()

    def arrived(slot, lanes):
        target = held.at[slot, :, :, :, :, pl.ds(0, lanes)]
        pltpu.make_async_copy(target, target, x_sem.at[slot]).wait()

    def send(b, outs, block):
        for k, source in enumerate((kept, sent)):
            pltpu.make_async_copy(source.at[b], outs[k].at[:, block], out_sem.at[b, k]).start()

    @pl.when(step == 0)
    def _():
        for k in range(2):
            target = held.at[0, :, :, core if k == 0 else 1 - core, :, pl.ds(0, half)]
            pltpu.make_async_copy(far_a[k], target, x_sem.at[0]).start()
        for k in range(w_sem.shape[0]):
            w_copy(k).start()
        fetch_b(0, 1)
        arrived(0, half)
        tokens = held[0, :, :, :, :, :half].reshape(depth, half)
        for k in range(w_sem.shape[0]):
            w_copy(k).wait()
            rows = slice(ROW_BLOCK * k, min(columns, ROW_BLOCK * (k + 1)))
            logits[rows, :] = jnp.dot(weights[rows, :], tokens, preferred_element_type=jnp.float32)

        def store(pieces, stats):
            write((kept.at[0], sent.at[0]), pieces, stats, core)

        summarise(logits[...], table_ref[...], core, store)
        send(0, outs_a, lax.rem(z + 2, SIDE))

    @pl.when(step > 0)
    def _():
        slot = lax.rem(step, 2)

        @pl.when(step == 1)
        def _():
            fetch_b(1, 0)

        arrived(slot, 2 * half)
        tokens = held[slot].reshape(depth, 2 * half)
        product = jnp.dot(weights[...], tokens, preferred_element_type=jnp.float32)

        def store(pieces, stats):
            for h in range(2):
                part = slice(groups * h, groups * h + groups)
                b = 2 * step - 1 + h
                write((kept.at[b], sent.at[b]), pieces[part], [kind[part] for kind in stats], core)
                send(b, outs_b, 2 * step - 2 + h)

        summarise(product, table_ref[...], core, store)

    @pl.when(step == pl.num_programs(0) - 1)
    def _():
        for b in range(5):
            for k, source in enumerate((kept, sent)):
                pltpu.make_async_copy(source.at[b], source.at[b], out_sem.at[b, k]).wait()


def finish(weights, table, far_a, part_b, previous):
    columns, depth = weights.shape
    features, half = far_a[0].shape[2:]
    rows = message_rows(half)
    shape = jax.ShapeDtypeStruct((PLANE, SIDE, rows, LANES), jnp.float32)
    results = pl.pallas_call(
        finish_kernel,
        grid=(3,),
        in_specs=[ANY, pl.BlockSpec(table.shape, lambda i: (0, 0))] + [ANY] * 12,
        out_specs=[ANY] * 4,
        out_shape=[shape] * 4,
        input_output_aliases={12: 0, 13: 1},
        scratch_shapes=[
            pltpu.VMEM((columns, depth), jnp.bfloat16),
            pltpu.VMEM((2, SIDE, SIDE, CORES, features, 2 * half), jnp.bfloat16),
            pltpu.VMEM((columns, half), jnp.float32),
            pltpu.VMEM((5, PLANE, rows, LANES), jnp.float32),
            pltpu.VMEM((5, PLANE, rows, LANES), jnp.float32),
            pltpu.SemaphoreType.DMA((pl.cdiv(columns, ROW_BLOCK),)),
            pltpu.SemaphoreType.DMA((2,)),
            pltpu.SemaphoreType.DMA((5, 2)),
        ],
        compiler_params=pltpu.CompilerParams(vmem_limit_bytes=VMEM_BYTES),
        cost_estimate=pl.CostEstimate(
            flops=2 * columns * (depth + B) * 5 * half,
            bytes_accessed=2 * depth * (columns + 5 * half),
            transcendentals=columns * 5 * half,
        ),
    )(weights, table, *far_a, *part_b, *previous)
    return results[:2], results[2:]


def unpack(message, groups):
    lead = message.shape[:-2]
    sums = message[..., : OWN * groups, :].reshape(*lead, groups, OWN, LANES)
    stats = message[..., OWN * groups :, :].reshape(*lead, KINDS, groups, LANES)
    return sums, [stats[..., k, :, :] for k in range(KINDS)]


def merge(kept, received, groups):
    sums_a, (high_a, low_a, *total_a) = unpack(kept, groups)
    sums_b, (high_b, low_b, *total_b) = unpack(received, groups)
    larger = high_a + low_a >= high_b + low_b
    high = jnp.where(larger, high_a, high_b)
    low = jnp.where(larger, low_a, low_b)
    scale_a = jnp.exp(high_a + low_a - (high + low))
    scale_b = jnp.exp(high_b + low_b - (high + low))
    sums = sums_a * scale_a[..., None, :] + sums_b * scale_b[..., None, :]
    total = (total_a[0] + total_a[1]) * scale_a + (total_b[0] + total_b[1]) * scale_b
    total_high = lax.reduce_precision(total, 8, 7)
    lead = kept.shape[:-2]
    return [sums.reshape(*lead, OWN * groups, LANES), high, low, total_high, total - total_high]


def per_device(hidden_states, head_weight, sign_bits, bucket_ids):
    width, features = hidden_states.shape
    half = width // 2
    groups = half // LANES
    weights = head_weight.T
    columns = weights.shape[0]
    buckets = lax.broadcasted_iota(jnp.int32, (B, columns), 0)
    table = jnp.where(buckets == bucket_ids[None, :], 2 * sign_bits[None, :] - 1, 0).astype(jnp.bfloat16)

    part_a, part_b = place(place_first_kernel, around(hidden_states.T, Y), (SIDE, features, half))
    own = place(place_second_kernel, around(part_a, X) + around(part_b, Z), (SIDE, SIDE, features, half))
    near = [ring(p, a) for p, a in zip(own, (Z, X))]
    other = [swap(p) for p in own]
    message_a = whole_blocks(weights, table, ("own",), (own[0], other[0]), ())
    other, message_a = lax.optimization_barrier((other, message_a))
    near_other = [ring(p, a) for p, a in zip(other, (Z, X))]
    near = lax.optimization_barrier(near)
    near_other = lax.optimization_barrier(near_other)
    far = [ring(p, a) for p, a in zip(near, (Z, X))]
    back = [swap(p) for p in near]
    back_other = [swap(p) for p in near_other]
    message_a = whole_blocks(weights, table, ("near", "back"), (near[0], near_other[0], back[0], back_other[0]), message_a)
    far, back, back_other, message_a = lax.optimization_barrier((far, back, back_other, message_a))
    far_other = [swap(p) for p in far]
    part_b = (own[1], other[1], near[1], near_other[1], back[1], back_other[1], far[1], far_other[1])
    message_a, message_b = finish(weights, table, (far[0], far_other[0]), part_b, message_a)

    pieces = []
    for kept, sent in (message_a, message_b):
        pieces += merge(kept, swap(sent), groups)
    packed = jnp.concatenate(pieces, axis=2).astype(jnp.float16)
    teams = [[device_at(x, y, z, c) for x in range(SIDE) for y in range(SIDE) for z in range(SIDE)] for c in range(CORES)]
    packed = packed.reshape(PLANE * SIDE, packed.shape[2], LANES)
    received = lax.all_to_all(packed, BOTH, 0, 0, axis_index_groups=teams, tiled=True).astype(jnp.float32)
    sums, (high, low, *totals) = unpack(received.reshape(PLANE * SIDE, 2, -1, LANES), groups)
    local_max = high + low
    rescale = jnp.exp(local_max - jnp.max(local_max, axis=0))
    row_total = jnp.sum((totals[0] + totals[1]) * rescale, axis=0)
    bucket_sums = jnp.sum(sums * rescale[..., None, :], axis=0)
    factor = jnp.sqrt(jnp.float32(V) * jnp.float32(B))
    sketch = bucket_sums / row_total[..., None, :] * factor
    return (sketch.transpose(0, 1, 3, 2).reshape(width, OWN), -jnp.log(row_total).reshape(width))


def solution(mesh):
    return jax.shard_map(
        per_device,
        mesh=mesh,
        in_specs=(
            P("rows", "vocab"),
            P(None, ("vocab", "rows")),
            P(("vocab", "rows")),
            P(("vocab", "rows")),
        ),
        out_specs=(P("rows", "vocab"), P("rows")),
        check_vma=False,
    )
```

time: 372 us -> 164 us (0.44)
  blocking collectives: 147 us -> 29.1 us
  waiting for transfers between devices: 161 us -> 55.5 us
  Pallas kernels: 0 us -> 45.3 us
  matrix products: 42.2 us -> 0 us
  starting transfers between devices: 0.12 us -> 25.6 us
  between operations: 13.8 us -> 0.91 us
  other arithmetic: 7.88 us -> 3.3 us
  local copies, waits for them, and re-layouts: 0.01 us -> 3.8 us
    all_gather x1 -> x0, waiting for transfers between devices: 81.4 us -> none  [per_device(): lax.all_gather(gathered_rows, 'vocab', axis=1, tiled=True)]
    reduce_scatter x2 -> x0, waiting for transfers between devices: 79.1 us -> none  [the longest x1 79.1 us: per_device(): lax.psum_scatter(partial_value, 'vocab', scatter_dimension=1, tiled=True)]
    pmax x1 -> x0, blocking collectives: 65 us -> none  [per_device(): row_max = lax.pmax(jnp.max(logits, axis=1), ('vocab', 'rows'))]
    psum x1 -> x0, blocking collectives: 64.9 us -> none  [per_device(): row_total = lax.psum(jnp.sum(exponent, axis=1), ('vocab', 'rows'))]
    ppermute x0 -> x25, waiting for transfers between devices: none -> 55.5 us  [permute(): return lax.ppermute(array, BOTH, pairs)]
    pallas_call x0 -> x5, Pallas kernels: none -> 45.3 us  [the longest x1 25.7 us: finish(): pl.pallas_call(finish_kernel, grid=(3,), in_specs=[ANY, pl.BlockSpec(tabl...]
    dot_general x2 -> x0, matrix products: 42.2 us -> none  [the longest x1 33.5 us: per_device(): jnp.dot(lax.all_gather(gathered_rows, 'vocab', axis=1, tiled=True), head_...]
    all_to_all x0 -> x1, blocking collectives: none -> 29.1 us  [per_device(): lax.all_to_all(packed, BOTH, 0, 0, axis_index_groups=teams, tiled=True)]
  transfers between devices with their start and end apart: 3 -> 25, of which waited for: 2 -> 17; matrix products, arithmetic and copies ran while one was open for 2% -> 0% of each run, Pallas kernels for 0% -> 11%
where the time goes in v2:
time: 164 us
  waiting for transfers between devices  55.5 us (34%)
  Pallas kernels  45.3 us (28%)
  blocking collectives  29.1 us (18%)
  starting transfers between devices  25.6 us (16%)
  local copies, waits for them, and re-layouts  3.8 us (2%)
  other arithmetic  3.3 us (2%)
    ppermute x25, waiting for transfers between devices, permute(): return lax.ppermute(array, BOTH, pairs)  55.5 us
    all_to_all x1, blocking collectives, per_device(): lax.all_to_all(packed, BOTH, 0, 0, axis_index_groups=teams, tiled=True)  29.1 us
    pallas_call x1, Pallas kernels, finish(): pl.pallas_call(finish_kernel, grid=(3,), in_specs=[ANY, pl.BlockSpec(tabl...  25.7 us
    ppermute x25, starting transfers between devices, permute(): return lax.ppermute(array, BOTH, pairs)  25.6 us
    pallas_call x2, Pallas kernels, whole_blocks(): pl.pallas_call(functools.partial(whole_kernel, which=which), grid=(steps,...  18.6 us
  transfers between devices with their start and end apart: 25, of which 17 were waited for; matrix products, arithmetic and copies ran while one was open for 0% of the time, Pallas kernels for 11%

profile of v2, /device:TPU:0, one launch (start us, length us, event | category | flops | bytes accessed | tf_op | source)
XLA Modules:
  0.0 163.5 jit_solution(15538917055504996680)
XLA Ops:
  0.6 3.4 %collective-permute-start.2 = (bf16[160,512]{1,0:T(8,128)(2,1)}, bf16[160,512]{1,0:T(8,128)(2,1)S(1)}, u32[]{:S(2)}, u32[]{:S(2)}) collective-permute-start(bf16[160,512]{1,0:T(8,128)(2,1)} %bitcast.370), channel_id=1, source_target_pairs={{0,16},{1,17},{2,18},{3,19},{4,20},{5,21},{6,22},{7,23},{8,24},{9,... | collective-permute-start | bytes 491528 | tf_op jit(solution)/shard_map/ppermute | solution.py:39
  4.0 1.1 collective-permute-start.1
  5.0 1.0 collective-permute-start
  6.0 3.5 %collective-permute-done.2.far = bf16[160,512]{1,0:T(8,128)(2,1)S(1)} collective-permute-done((bf16[160,512]{1,0:T(8,128)(2,1)}, bf16[160,512]{1,0:T(8,128)(2,1)S(1)}, u32[]{:S(2)}, u32[]{:S(2)}) %collective-permute-start.2) | collective-permute-done | bytes 163872 | tf_op jit(solution)/shard_map/ppermute | solution.py:39
  9.5 2.8 %collective-permute-done.1.upper = bf16[160,512]{1,0:T(8,128)(2,1)S(1)} collective-permute-done((bf16[160,512]{1,0:T(8,128)(2,1)}, bf16[160,512]{1,0:T(8,128)(2,1)S(1)}, u32[]{:S(2)}, u32[]{:S(2)}) %collective-permute-start.1) | collective-permute-done | bytes 163872 | tf_op jit(solution)/shard_map/ppermute | solution.py:39
  12.3 0.1 collective-permute-done.lower
  12.4 0.9 copy-done
  13.3 0.1 shard_map.59
  13.5 3.1 %collective-permute-start.5 = (bf16[4,160,256]{2,1,0:T(8,128)(2,1)S(1)}, bf16[4,160,256]{2,1,0:T(8,128)(2,1)S(1)}, u32[]{:S(2)}, u32[]{:S(2)}) collective-permute-start(bf16[4,160,256]{2,1,0:T(8,128)(2,1)S(1)} %get-tuple-element.28.refs_0_), channel_id=1, source_target_pairs={{0,64},{1,65},{2,66},{3,67},{4,68},{5,69},{6,70},{7,71},{8,72},{9,... | collective-permute-start | bytes 983048 | tf_op jit(solution)/shard_map/ppermute | solution.py:39
  16.6 1.1 collective-permute-start.4
  17.8 0.9 collective-permute-start.3
  18.7 3.9 %collective-permute-start.8 = (bf16[4,160,256]{2,1,0:T(8,128)(2,1)S(1)}, bf16[4,160,256]{2,1,0:T(8,128)(2,1)S(1)}, u32[]{:S(2)}, u32[]{:S(2)}) collective-permute-start(bf16[4,160,256]{2,1,0:T(8,128)(2,1)S(1)} %get-tuple-element.29.refs_4_), channel_id=1, source_target_pairs={{0,2},{1,3},{2,0},{3,1},{4,6},{5,7},{6,4},{7,5},{8,10},{9,11},{10,... | collective-permute-start | bytes 983048 | tf_op jit(solution)/shard_map/ppermute | solution.py:39
  22.6 0.7 collective-permute-start.7
  23.3 2.5 %collective-permute-done.5.refs_3_ = bf16[4,160,256]{2,1,0:T(8,128)(2,1)S(1)} collective-permute-done((bf16[4,160,256]{2,1,0:T(8,128)(2,1)S(1)}, bf16[4,160,256]{2,1,0:T(8,128)(2,1)S(1)}, u32[]{:S(2)}, u32[]{:S(2)}) %collective-permute-start.5) | collective-permute-done | bytes 327712 | tf_op jit(solution)/shard_map/ppermute | solution.py:39
  25.7 2.0 %collective-permute-start.6 = (bf16[4,160,256]{2,1,0:T(8,128)(2,1)S(1)}, bf16[4,160,256]{2,1,0:T(8,128)(2,1)S(1)}, u32[]{:S(2)}, u32[]{:S(2)}) collective-permute-start(bf16[4,160,256]{2,1,0:T(8,128)(2,1)S(1)} %get-tuple-element.29.refs_4_), channel_id=1, source_target_pairs={{0,1},{1,2},{2,3},{3,0},{4,5},{5,6},{6,7},{7,4},{8,9},{9,10},{10,1... | collective-permute-start | bytes 983048 | tf_op jit(solution)/shard_map/ppermute | solution.py:39
  27.7 3.2 %collective-permute-done.4.refs_2_ = bf16[4,160,256]{2,1,0:T(8,128)(2,1)S(1)} collective-permute-done((bf16[4,160,256]{2,1,0:T(8,128)(2,1)S(1)}, bf16[4,160,256]{2,1,0:T(8,128)(2,1)S(1)}, u32[]{:S(2)}, u32[]{:S(2)}) %collective-permute-start.4) | collective-permute-done | bytes 327712 | tf_op jit(solution)/shard_map/ppermute | solution.py:39
  30.9 5.5 %collective-permute-done.7.refs_6_ = bf16[4,160,256]{2,1,0:T(8,128)(2,1)S(1)} collective-permute-done((bf16[4,160,256]{2,1,0:T(8,128)(2,1)S(1)}, bf16[4,160,256]{2,1,0:T(8,128)(2,1)S(1)}, u32[]{:S(2)}, u32[]{:S(2)}) %collective-permute-start.7) | collective-permute-done | bytes 327712 | tf_op jit(solution)/shard_map/ppermute | solution.py:39
  36.4 0.0 collective-permute-done.6.refs_5_
  36.4 0.9 shard_map.60
  37.3 0.1 collective-permute-start.15
  37.4 0.5 collective-permute-start.16
  37.9 1.0 collective-permute-start.9
  38.9 0.6 collective-permute-start.10
  39.5 0.4 select_convert_fusion.table_ref
  39.9 0.6 collective-permute-done.15.refs_1_
  40.4 7.8 %shard_map.61 = (f32[16,4,40,128]{3,2,1,0:T(8,128)S(1)}, f32[16,4,40,128]{3,2,1,0:T(8,128)S(1)}) custom-call(bf16[1187,5120]{1,0:T(8,128)(2,1)} %bitcast.374, bf16[512,1187]{1,0:T(8,128)(2,1)S(1)} %select_convert_fusion.table_ref, bf16[4,4,160,256]{3,2,1,0:T(8,128)(2,1)S(1)} %get-tuple-element.30.refs_0_, ...), custom_call_target="tpu_custom_call" | custom-call | flops 3422814208 | bytes 14776320 | tf_op jit(solution)/shard_map/pallas_call | solution.py:206
  48.3 1.1 collective-permute-start.17
  49.4 0.5 collective-permute-start.18
  49.9 6.8 %collective-permute-done.9.refs_0_ = bf16[4,4,160,256]{3,2,1,0:T(8,128)(2,1)S(1)} collective-permute-done((bf16[4,4,160,256]{3,2,1,0:T(8,128)(2,1)S(1)}, bf16[4,4,160,256]{3,2,1,0:T(8,128)(2,1)S(1)}, u32[]{:S(2)}, u32[]{:S(2)}) %collective-permute-start.9) | collective-permute-done | bytes 1310752 | tf_op jit(solution)/shard_map/ppermute | solution.py:39
  56.7 1.0 collective-permute-done.10.refs_4_
  57.7 13.1 %collective-permute-done.17.refs_1_ = bf16[4,4,160,256]{3,2,1,0:T(8,128)(2,1)S(1)} collective-permute-done((bf16[4,4,160,256]{3,2,1,0:T(8,128)(2,1)S(1)}, bf16[4,4,160,256]{3,2,1,0:T(8,128)(2,1)S(1)}, u32[]{:S(2)}, u32[]{:S(2)}) %collective-permute-start.17) | collective-permute-done | bytes 1310752 | tf_op jit(solution)/shard_map/ppermute | solution.py:39
  70.8 1.0 collective-permute-done.18.refs_5_
  71.7 1.5 collective-permute-start.11
  73.2 1.0 collective-permute-start.14
  74.3 0.9 collective-permute-start.20
  75.1 10.7 %shard_map.62 = (f32[16,4,40,128]{3,2,1,0:T(8,128)S(1)}, f32[16,4,40,128]{3,2,1,0:T(8,128)S(1)}) custom-call(bf16[1187,5120]{1,0:T(8,128)(2,1)} %bitcast.375, bf16[512,1187]{1,0:T(8,128)(2,1)S(1)} %select_convert_fusion.table_ref, bf16[4,4,160,256]{3,2,1,0:T(8,128)(2,1)S(1)} %collective-permute-done.9.refs_0_, ...), custom_call_target="tpu_custom_call", output_to_operand_aliasing={{0}: (6, {}), {1}: (7, {})} | custom-call | flops 6845628416 | bytes 17397760 | tf_op jit(solution)/shard_map/pallas_call | solution.py:206
  85.9 4.7 %collective-permute-done.11.refs_0_ = bf16[4,4,160,256]{3,2,1,0:T(8,128)(2,1)S(1)} collective-permute-done((bf16[4,4,160,256]{3,2,1,0:T(8,128)(2,1)S(1)}, bf16[4,4,160,256]{3,2,1,0:T(8,128)(2,1)S(1)}, u32[]{:S(2)}, u32[]{:S(2)}) %collective-permute-start.11) | collective-permute-done | bytes 1310752 | tf_op jit(solution)/shard_map/ppermute | solution.py:39
  90.6 2.5 %collective-permute-done.12.refs_8_ = bf16[4,4,160,256]{3,2,1,0:T(8,128)(2,1)S(1)} collective-permute-done((bf16[4,4,160,256]{3,2,1,0:T(8,128)(2,1)S(1)}, bf16[4,4,160,256]{3,2,1,0:T(8,128)(2,1)S(1)}, u32[]{:S(2)}, u32[]{:S(2)}) %collective-permute-start.12) | collective-permute-done | bytes 1310752 | tf_op jit(solution)/shard_map/ppermute | solution.py:39
  93.1 0.3 collective-permute-start.21
  93.3 0.5 collective-permute-start.22
  93.8 2.5 %collective-permute-done.21.refs_1_ = bf16[4,4,160,256]{3,2,1,0:T(8,128)(2,1)S(1)} collective-permute-done((bf16[4,4,160,256]{3,2,1,0:T(8,128)(2,1)S(1)}, bf16[4,4,160,256]{3,2,1,0:T(8,128)(2,1)S(1)}, u32[]{:S(2)}, u32[]{:S(2)}) %collective-permute-start.21) | collective-permute-done | bytes 1310752 | tf_op jit(solution)/shard_map/ppermute | solution.py:39
  96.4 1.9 %collective-permute-done.22.refs_9_ = bf16[4,4,160,256]{3,2,1,0:T(8,128)(2,1)S(1)} collective-permute-done((bf16[4,4,160,256]{3,2,1,0:T(8,128)(2,1)S(1)}, bf16[4,4,160,256]{3,2,1,0:T(8,128)(2,1)S(1)}, u32[]{:S(2)}, u32[]{:S(2)}) %collective-permute-start.22) | collective-permute-done | bytes 1310752 | tf_op jit(solution)/shard_map/ppermute | solution.py:39
  98.3 1.1 copy-done.10
  99.3 25.7 %shard_map.63 = (f32[16,4,40,128]{3,2,1,0:T(8,128)S(1)}, f32[16,4,40,128]{3,2,1,0:T(8,128)S(1)}, f32[16,4,40,128]{3,2,1,0:T(8,128)S(1)}, f32[16,4,40,128]{3,2,1,0:T(8,128)S(1)}) custom-call(bf16[1187,5120]{1,0:T(8,128)(2,1)} %bitcast.376, bf16[512,1187]{1,0:T(8,128)(2,1)S(1)} %select_convert_fusion.table_ref, ...), custom_call_target="tpu_custom_call", output_to_operand_aliasing={{0}: (12, {}), {1}: (13, {})} | custom-call | flops 17114071040 | bytes 25262080 | tf_op jit(solution)/shard_map/pallas_call | solution.py:316
  125.0 0.2 collective-permute-start.23
  125.2 0.4 collective-permute-start.24
  125.7 2.5 %collective-permute-done.23 = f32[16,4,40,128]{3,2,1,0:T(8,128)S(1)} collective-permute-done((f32[16,4,40,128]{3,2,1,0:T(8,128)S(1)}, f32[16,4,40,128]{3,2,1,0:T(8,128)S(1)}, u32[]{:S(2)}, u32[]{:S(2)}) %collective-permute-start.23) | collective-permute-done | bytes 1310752 | tf_op jit(solution)/shard_map/ppermute | solution.py:39
  128.2 0.1 fusion.17
  128.3 0.2 slice_add_fusion.3
  128.5 1.6 collective-permute-done.24
  130.0 0.1 fusion.14
  130.2 0.2 slice_add_fusion.1
  130.3 0.2 fusion.10
  130.6 0.2 fusion.11
  130.9 0.2 fusion.4
  131.1 0.2 fusion.2
  131.4 1.0 concatenate.11
  132.4 29.1 %all_to_all.5 = f16[64,80,128]{2,1,0:T(8,128)(2,1)S(1)} all-to-all(f16[64,80,128]{2,1,0:T(8,128)(2,1)S(1)} %concatenate.11), channel_id=1, replica_groups={{0,1,2,3,8,9,10,11,16,17,18,19,24,25,26,27,32,33,34,35,40,41,42,43,48,4..., dimensions={0} | all-to-all | bytes 2621440 | tf_op jit(solution)/shard_map/all_to_all | solution.py:398
  161.4 0.2 convert.43
  161.7 0.1 fusion.30
  161.8 0.2 fusion.9
  162.0 0.3 fusion
  162.3 0.6 log_negate_fusion
  162.9 0.6 reshape.252
  (40 shorter events, 0.3 us)
Async XLA Ops:
  0.6 8.9 %collective-permute-start.2 = (bf16[160,512]{1,0:T(8,128)(2,1)}, bf16[160,512]{1,0:T(8,128)(2,1)S(1)}, u32[]{:S(2)}, u32[]{:S(2)}) collective-permute-start(bf16[160,512]{1,0:T(8,128)(2,1)} %bitcast.370), channel_id=1, source_target_pairs={{0,16},{1,17},{2,18},{3,19},{4,20},{5,21},{6,22},{7,23},{8,24},{9,... | collective-permute-start | bytes 491528 | tf_op jit(solution)/shard_map/ppermute | solution.py:39
  4.0 8.3 %collective-permute-start.1 = (bf16[160,512]{1,0:T(8,128)(2,1)}, bf16[160,512]{1,0:T(8,128)(2,1)S(1)}, u32[]{:S(2)}, u32[]{:S(2)}) collective-permute-start(bf16[160,512]{1,0:T(8,128)(2,1)} %bitcast.371), channel_id=1, source_target_pairs={{0,24},{1,25},{2,26},{3,27},{4,28},{5,29},{6,30},{7,31},{8,0},{9,1... | collective-permute-start | bytes 491528 | tf_op jit(solution)/shard_map/ppermute | solution.py:39
  5.0 7.4 %collective-permute-start = (bf16[160,512]{1,0:T(8,128)(2,1)}, bf16[160,512]{1,0:T(8,128)(2,1)S(1)}, u32[]{:S(2)}, u32[]{:S(2)}) collective-permute-start(bf16[160,512]{1,0:T(8,128)(2,1)} %bitcast.372), channel_id=1, source_target_pairs={{0,8},{1,9},{2,10},{3,11},{4,12},{5,13},{6,14},{7,15},{8,16},{9,17... | collective-permute-start | bytes 491528 | tf_op jit(solution)/shard_map/ppermute | solution.py:39
  12.4 0.9 copy-start
  13.5 12.2 %collective-permute-start.5 = (bf16[4,160,256]{2,1,0:T(8,128)(2,1)S(1)}, bf16[4,160,256]{2,1,0:T(8,128)(2,1)S(1)}, u32[]{:S(2)}, u32[]{:S(2)}) collective-permute-start(bf16[4,160,256]{2,1,0:T(8,128)(2,1)S(1)} %get-tuple-element.28.refs_0_), channel_id=1, source_target_pairs={{0,64},{1,65},{2,66},{3,67},{4,68},{5,69},{6,70},{7,71},{8,72},{9,... | collective-permute-start | bytes 983048 | tf_op jit(solution)/shard_map/ppermute | solution.py:39
  16.6 14.2 %collective-permute-start.4 = (bf16[4,160,256]{2,1,0:T(8,128)(2,1)S(1)}, bf16[4,160,256]{2,1,0:T(8,128)(2,1)S(1)}, u32[]{:S(2)}, u32[]{:S(2)}) collective-permute-start(bf16[4,160,256]{2,1,0:T(8,128)(2,1)S(1)} %get-tuple-element.28.refs_0_), channel_id=1, source_target_pairs={{0,96},{1,97},{2,98},{3,99},{4,100},{5,101},{6,102},{7,103},{8,104... | collective-permute-start | bytes 983048 | tf_op jit(solution)/shard_map/ppermute | solution.py:39
  17.8 13.1 %collective-permute-start.3 = (bf16[4,160,256]{2,1,0:T(8,128)(2,1)S(1)}, bf16[4,160,256]{2,1,0:T(8,128)(2,1)S(1)}, u32[]{:S(2)}, u32[]{:S(2)}) collective-permute-start(bf16[4,160,256]{2,1,0:T(8,128)(2,1)S(1)} %get-tuple-element.28.refs_0_), channel_id=1, source_target_pairs={{0,32},{1,33},{2,34},{3,35},{4,36},{5,37},{6,38},{7,39},{8,40},{9,... | collective-permute-start | bytes 983048 | tf_op jit(solution)/shard_map/ppermute | solution.py:39
  18.7 19.2 %copy-start.2 = (s32[1187]{0:T(1024)S(1)}, s32[1187]{0:T(1024)}, u32[]{:S(2)}) copy-start(s32[1187]{0:T(1024)} %param.6) | copy-start | bytes 14248
  18.7 20.8 %copy-start.3 = (s32[1187]{0:T(1024)S(1)}, s32[1187]{0:T(1024)}, u32[]{:S(2)}) copy-start(s32[1187]{0:T(1024)} %param.7) | copy-start | bytes 14248
  18.7 12.2 %collective-permute-start.8 = (bf16[4,160,256]{2,1,0:T(8,128)(2,1)S(1)}, bf16[4,160,256]{2,1,0:T(8,128)(2,1)S(1)}, u32[]{:S(2)}, u32[]{:S(2)}) collective-permute-start(bf16[4,160,256]{2,1,0:T(8,128)(2,1)S(1)} %get-tuple-element.29.refs_4_), channel_id=1, source_target_pairs={{0,2},{1,3},{2,0},{3,1},{4,6},{5,7},{6,4},{7,5},{8,10},{9,11},{10,... | collective-permute-start | bytes 983048 | tf_op jit(solution)/shard_map/ppermute | solution.py:39
  22.6 13.8 %collective-permute-start.7 = (bf16[4,160,256]{2,1,0:T(8,128)(2,1)S(1)}, bf16[4,160,256]{2,1,0:T(8,128)(2,1)S(1)}, u32[]{:S(2)}, u32[]{:S(2)}) collective-permute-start(bf16[4,160,256]{2,1,0:T(8,128)(2,1)S(1)} %get-tuple-element.29.refs_4_), channel_id=1, source_target_pairs={{0,3},{1,0},{2,1},{3,2},{4,7},{5,4},{6,5},{7,6},{8,11},{9,8},{10,9... | collective-permute-start | bytes 983048 | tf_op jit(solution)/shard_map/ppermute | solution.py:39
  25.7 10.6 %collective-permute-start.6 = (bf16[4,160,256]{2,1,0:T(8,128)(2,1)S(1)}, bf16[4,160,256]{2,1,0:T(8,128)(2,1)S(1)}, u32[]{:S(2)}, u32[]{:S(2)}) collective-permute-start(bf16[4,160,256]{2,1,0:T(8,128)(2,1)S(1)} %get-tuple-element.29.refs_4_), channel_id=1, source_target_pairs={{0,1},{1,2},{2,3},{3,0},{4,5},{5,6},{6,7},{7,4},{8,9},{9,10},{10,1... | collective-permute-start | bytes 983048 | tf_op jit(solution)/shard_map/ppermute | solution.py:39
  37.3 11.0 %copy-start.1 = (bf16[4,4,160,256]{3,2,1,0:T(8,128)(2,1)}, bf16[4,4,160,256]{3,2,1,0:T(8,128)(2,1)S(1)}, u32[]{:S(2)}) copy-start(bf16[4,4,160,256]{3,2,1,0:T(8,128)(2,1)S(1)} %get-tuple-element.31.refs_2_) | copy-start | bytes 3932164
  37.3 3.1 %collective-permute-start.15 = (bf16[4,4,160,256]{3,2,1,0:T(8,128)(2,1)S(1)}, bf16[4,4,160,256]{3,2,1,0:T(8,128)(2,1)S(1)}, u32[]{:S(2)}, u32[]{:S(2)}) collective-permute-start(bf16[4,4,160,256]{3,2,1,0:T(8,128)(2,1)S(1)} %get-tuple-element.30.refs_0_), channel_id=1, source_target_pairs={{0,4},{1,5},{2,6},{3,7},{4,0},{5,1},{6,2},{7,3},{8,12},{9,13},{10,... | collective-permute-start | bytes 3932168 | tf_op jit(solution)/shard_map/ppermute | solution.py:39
  37.4 10.9 %collective-permute-start.16 = (bf16[4,4,160,256]{3,2,1,0:T(8,128)(2,1)S(1)}, bf16[4,4,160,256]{3,2,1,0:T(8,128)(2,1)S(1)}, u32[]{:S(2)}, u32[]{:S(2)}) collective-permute-start(bf16[4,4,160,256]{3,2,1,0:T(8,128)(2,1)S(1)} %get-tuple-element.31.refs_2_), channel_id=1, source_target_pairs={{0,4},{1,5},{2,6},{3,7},{4,0},{5,1},{6,2},{7,3},{8,12},{9,13},{10,... | collective-permute-start | bytes 3932168 | tf_op jit(solution)/shard_map/ppermute | solution.py:39
  37.9 18.8 %collective-permute-start.9 = (bf16[4,4,160,256]{3,2,1,0:T(8,128)(2,1)S(1)}, bf16[4,4,160,256]{3,2,1,0:T(8,128)(2,1)S(1)}, u32[]{:S(2)}, u32[]{:S(2)}) collective-permute-start(bf16[4,4,160,256]{3,2,1,0:T(8,128)(2,1)S(1)} %get-tuple-element.30.refs_0_), channel_id=1, source_target_pairs={{0,1},{1,2},{2,3},{3,0},{4,7},{5,4},{6,5},{7,6},{8,9},{9,10},{10,1... | collective-permute-start | bytes 3932168 | tf_op jit(solution)/shard_map/ppermute | solution.py:39
  38.9 18.8 %collective-permute-start.10 = (bf16[4,4,160,256]{3,2,1,0:T(8,128)(2,1)S(1)}, bf16[4,4,160,256]{3,2,1,0:T(8,128)(2,1)S(1)}, u32[]{:S(2)}, u32[]{:S(2)}) collective-permute-start(bf16[4,4,160,256]{3,2,1,0:T(8,128)(2,1)S(1)} %get-tuple-element.31.refs_2_), channel_id=1, source_target_pairs={{0,32},{1,33},{2,34},{3,35},{4,100},{5,101},{6,102},{7,103},{8,40}... | collective-permute-start | bytes 3932168 | tf_op jit(solution)/shard_map/ppermute | solution.py:39
  48.3 37.6 %copy-start.4 = (bf16[4,4,160,256]{3,2,1,0:T(8,128)(2,1)}, bf16[4,4,160,256]{3,2,1,0:T(8,128)(2,1)S(1)}, u32[]{:S(2)}) copy-start(bf16[4,4,160,256]{3,2,1,0:T(8,128)(2,1)S(1)} %collective-permute-done.16.refs_3_) | copy-start | bytes 3932164
  48.3 22.5 %collective-permute-start.17 = (bf16[4,4,160,256]{3,2,1,0:T(8,128)(2,1)S(1)}, bf16[4,4,160,256]{3,2,1,0:T(8,128)(2,1)S(1)}, u32[]{:S(2)}, u32[]{:S(2)}) collective-permute-start(bf16[4,4,160,256]{3,2,1,0:T(8,128)(2,1)S(1)} %collective-permute-done.15.refs_1_), channel_id=1, source_target_pairs={{0,1},{1,2},{2,3},{3,0},{4,7},{5,4},{6,5},{7,6},{8,9},{9,10},{10,1... | collective-permute-start | bytes 3932168 | tf_op jit(solution)/shard_map/ppermute | solution.py:39
  49.4 22.3 %collective-permute-start.18 = (bf16[4,4,160,256]{3,2,1,0:T(8,128)(2,1)S(1)}, bf16[4,4,160,256]{3,2,1,0:T(8,128)(2,1)S(1)}, u32[]{:S(2)}, u32[]{:S(2)}) collective-permute-start(bf16[4,4,160,256]{3,2,1,0:T(8,128)(2,1)S(1)} %collective-permute-done.16.refs_3_), channel_id=1, source_target_pairs={{0,32},{1,33},{2,34},{3,35},{4,100},{5,101},{6,102},{7,103},{8,40}... | collective-permute-start | bytes 3932168 | tf_op jit(solution)/shard_map/ppermute | solution.py:39
  57.7 28.2 %copy-start.5 = (bf16[4,4,160,256]{3,2,1,0:T(8,128)(2,1)}, bf16[4,4,160,256]{3,2,1,0:T(8,128)(2,1)S(1)}, u32[]{:S(2)}) copy-start(bf16[4,4,160,256]{3,2,1,0:T(8,128)(2,1)S(1)} %collective-permute-done.10.refs_4_) | copy-start | bytes 3932164
  57.7 16.6 %collective-permute-start.13 = (bf16[4,4,160,256]{3,2,1,0:T(8,128)(2,1)S(1)}, bf16[4,4,160,256]{3,2,1,0:T(8,128)(2,1)S(1)}, u32[]{:S(2)}, u32[]{:S(2)}) collective-permute-start(bf16[4,4,160,256]{3,2,1,0:T(8,128)(2,1)S(1)} %collective-permute-done.9.refs_0_), channel_id=1, source_target_pairs={{0,4},{1,5},{2,6},{3,7},{4,0},{5,1},{6,2},{7,3},{8,12},{9,13},{10,... | collective-permute-start | bytes 3932168 | tf_op jit(solution)/shard_map/ppermute | solution.py:39
  71.7 14.2 %copy-start.6 = (bf16[4,4,160,256]{3,2,1,0:T(8,128)(2,1)}, bf16[4,4,160,256]{3,2,1,0:T(8,128)(2,1)S(1)}, u32[]{:S(2)}) copy-start(bf16[4,4,160,256]{3,2,1,0:T(8,128)(2,1)S(1)} %collective-permute-done.18.refs_5_) | copy-start | bytes 3932164
  71.7 3.4 %collective-permute-start.19 = (bf16[4,4,160,256]{3,2,1,0:T(8,128)(2,1)S(1)}, bf16[4,4,160,256]{3,2,1,0:T(8,128)(2,1)S(1)}, u32[]{:S(2)}, u32[]{:S(2)}) collective-permute-start(bf16[4,4,160,256]{3,2,1,0:T(8,128)(2,1)S(1)} %collective-permute-done.17.refs_1_), channel_id=1, source_target_pairs={{0,4},{1,5},{2,6},{3,7},{4,0},{5,1},{6,2},{7,3},{8,12},{9,13},{10,... | collective-permute-start | bytes 3932168 | tf_op jit(solution)/shard_map/ppermute | solution.py:39
  71.7 18.8 %collective-permute-start.11 = (bf16[4,4,160,256]{3,2,1,0:T(8,128)(2,1)S(1)}, bf16[4,4,160,256]{3,2,1,0:T(8,128)(2,1)S(1)}, u32[]{:S(2)}, u32[]{:S(2)}) collective-permute-start(bf16[4,4,160,256]{3,2,1,0:T(8,128)(2,1)S(1)} %collective-permute-done.9.refs_0_), channel_id=1, source_target_pairs={{0,1},{1,2},{2,3},{3,0},{4,7},{5,4},{6,5},{7,6},{8,9},{9,10},{10,1... | collective-permute-start | bytes 3932168 | tf_op jit(solution)/shard_map/ppermute | solution.py:39
  73.2 17.4 %collective-permute-start.14 = (bf16[4,4,160,256]{3,2,1,0:T(8,128)(2,1)S(1)}, bf16[4,4,160,256]{3,2,1,0:T(8,128)(2,1)S(1)}, u32[]{:S(2)}, u32[]{:S(2)}) collective-permute-start(bf16[4,4,160,256]{3,2,1,0:T(8,128)(2,1)S(1)} %collective-permute-done.10.refs_4_), channel_id=1, source_target_pairs={{0,4},{1,5},{2,6},{3,7},{4,0},{5,1},{6,2},{7,3},{8,12},{9,13},{10,... | collective-permute-start | bytes 3932168 | tf_op jit(solution)/shard_map/ppermute | solution.py:39
  74.2 18.8 %collective-permute-start.12 = (bf16[4,4,160,256]{3,2,1,0:T(8,128)(2,1)S(1)}, bf16[4,4,160,256]{3,2,1,0:T(8,128)(2,1)S(1)}, u32[]{:S(2)}, u32[]{:S(2)}) collective-permute-start(bf16[4,4,160,256]{3,2,1,0:T(8,128)(2,1)S(1)} %collective-permute-done.10.refs_4_), channel_id=1, source_target_pairs={{0,32},{1,33},{2,34},{3,35},{4,100},{5,101},{6,102},{7,103},{8,40}... | collective-permute-start | bytes 3932168 | tf_op jit(solution)/shard_map/ppermute | solution.py:39
  74.3 18.8 %collective-permute-start.20 = (bf16[4,4,160,256]{3,2,1,0:T(8,128)(2,1)S(1)}, bf16[4,4,160,256]{3,2,1,0:T(8,128)(2,1)S(1)}, u32[]{:S(2)}, u32[]{:S(2)}) collective-permute-start(bf16[4,4,160,256]{3,2,1,0:T(8,128)(2,1)S(1)} %collective-permute-done.18.refs_5_), channel_id=1, source_target_pairs={{0,4},{1,5},{2,6},{3,7},{4,0},{5,1},{6,2},{7,3},{8,12},{9,13},{10,... | collective-permute-start | bytes 3932168 | tf_op jit(solution)/shard_map/ppermute | solution.py:39
  90.6 7.7 %copy-start.7 = (bf16[4,4,160,256]{3,2,1,0:T(8,128)(2,1)}, bf16[4,4,160,256]{3,2,1,0:T(8,128)(2,1)S(1)}, u32[]{:S(2)}) copy-start(bf16[4,4,160,256]{3,2,1,0:T(8,128)(2,1)S(1)} %collective-permute-done.14.refs_6_) | copy-start | bytes 3932164
  93.1 5.2 %copy-start.8 = (bf16[4,4,160,256]{3,2,1,0:T(8,128)(2,1)}, bf16[4,4,160,256]{3,2,1,0:T(8,128)(2,1)S(1)}, u32[]{:S(2)}) copy-start(bf16[4,4,160,256]{3,2,1,0:T(8,128)(2,1)S(1)} %collective-permute-done.12.refs_8_) | copy-start | bytes 3932164
  93.1 5.2 %copy-start.9 = (bf16[4,4,160,256]{3,2,1,0:T(8,128)(2,1)}, bf16[4,4,160,256]{3,2,1,0:T(8,128)(2,1)S(1)}, u32[]{:S(2)}) copy-start(bf16[4,4,160,256]{3,2,1,0:T(8,128)(2,1)S(1)} %collective-permute-done.20.refs_7_) | copy-start | bytes 3932164
  93.1 3.3 %collective-permute-start.21 = (bf16[4,4,160,256]{3,2,1,0:T(8,128)(2,1)S(1)}, bf16[4,4,160,256]{3,2,1,0:T(8,128)(2,1)S(1)}, u32[]{:S(2)}, u32[]{:S(2)}) collective-permute-start(bf16[4,4,160,256]{3,2,1,0:T(8,128)(2,1)S(1)} %collective-permute-done.11.refs_0_), channel_id=1, source_target_pairs={{0,4},{1,5},{2,6},{3,7},{4,0},{5,1},{6,2},{7,3},{8,12},{9,13},{10,... | collective-permute-start | bytes 3932168 | tf_op jit(solution)/shard_map/ppermute | solution.py:39
  93.3 4.9 %collective-permute-start.22 = (bf16[4,4,160,256]{3,2,1,0:T(8,128)(2,1)S(1)}, bf16[4,4,160,256]{3,2,1,0:T(8,128)(2,1)S(1)}, u32[]{:S(2)}, u32[]{:S(2)}) collective-permute-start(bf16[4,4,160,256]{3,2,1,0:T(8,128)(2,1)S(1)} %collective-permute-done.12.refs_8_), channel_id=1, source_target_pairs={{0,4},{1,5},{2,6},{3,7},{4,0},{5,1},{6,2},{7,3},{8,12},{9,13},{10,... | collective-permute-start | bytes 3932168 | tf_op jit(solution)/shard_map/ppermute | solution.py:39
  98.2 1.1 copy-start.10
  125.0 3.1 %collective-permute-start.23 = (f32[16,4,40,128]{3,2,1,0:T(8,128)S(1)}, f32[16,4,40,128]{3,2,1,0:T(8,128)S(1)}, u32[]{:S(2)}, u32[]{:S(2)}) collective-permute-start(f32[16,4,40,128]{3,2,1,0:T(8,128)S(1)} %get-tuple-element.51), channel_id=1, source_target_pairs={{0,4},{1,5},{2,6},{3,7},{4,0},{5,1},{6,2},{7,3},{8,12},{9,13},{10,... | collective-permute-start | bytes 3932168 | tf_op jit(solution)/shard_map/ppermute | solution.py:39
  125.2 4.8 %collective-permute-start.24 = (f32[16,4,40,128]{3,2,1,0:T(8,128)S(1)}, f32[16,4,40,128]{3,2,1,0:T(8,128)S(1)}, u32[]{:S(2)}, u32[]{:S(2)}) collective-permute-start(f32[16,4,40,128]{3,2,1,0:T(8,128)S(1)} %get-tuple-element.53), channel_id=1, source_target_pairs={{0,4},{1,5},{2,6},{3,7},{4,0},{5,1},{6,2},{7,3},{8,12},{9,13},{10,... | collective-permute-start | bytes 3932168 | tf_op jit(solution)/shard_map/ppermute | solution.py:39

commit v3 on v2

--- a/solution.py
+++ b/solution.py
@@ -48,10 +48,10 @@
     return permute(array, target)
 
 
-def ring(array, axis):
+def ring(array, axis, sign=1):
     def target(x, y, z, core):
         place = [x, y, z]
-        place[axis] = (place[axis] + (1 if core == 0 else -1)) % SIDE
+        place[axis] = (place[axis] + (sign if core == 0 else -sign)) % SIDE
         return (*place, core)
 
     return permute(array, target)
@@ -82,11 +82,11 @@
 
 
 def place_second_kernel(*refs):
-    coords, _ = position()
+    coords, core = position()
     outs, sem = refs[8:10], refs[10]
     copies = []
     for part, axis in enumerate((X, Z)):
-        for k, step in enumerate((0, -1, 1, 2)):
+        for k, step in enumerate((0, 2 * core - 1, 1 - 2 * core, 2)):
             slot = lax.rem(coords[axis] + SIDE + step, SIDE)
             copies.append(pltpu.make_async_copy(refs[4 * part + k], outs[part].at[slot], sem.at[4 * part + k]))
     for copy in copies:
@@ -109,20 +109,19 @@
     return (array, shift(array, axis, 1), shift(array, axis, -1), shift(array, axis, 2))
 
 
-def split_bf16(value):
-    high = value.astype(jnp.bfloat16).astype(jnp.float32)
-    low = (value - high).astype(jnp.bfloat16).astype(jnp.float32)
-    return high, low
+def around_by_ring(array, axis):
+    ahead = ring(array, axis)
+    return (array, ahead, ring(array, axis, -1), ring(ahead, axis))
 
 
 def summarise(logits, table, core, store):
-    max_high, max_low = split_bf16(jnp.max(logits, axis=0, keepdims=True))
-    exponent = jnp.exp(logits - (max_high + max_low))
-    total_high, total_low = split_bf16(jnp.sum(exponent, axis=0, keepdims=True))
+    local_max = jnp.max(logits, axis=0, keepdims=True)
+    exponent = jnp.exp(logits - local_max)
+    total = jnp.sum(exponent, axis=0, keepdims=True)
     sums = jnp.dot(table, exponent.astype(jnp.bfloat16), preferred_element_type=jnp.float32)
     groups = logits.shape[1] // LANES
     pieces = [sums[:, LANES * g : LANES * g + LANES].reshape(PLANE, CORES, OWN, LANES) for g in range(groups)]
-    kinds = (max_high, max_low, total_high, total_low)
+    kinds = (local_max, total, local_max, total)
     stats = [[kind[:, LANES * g : LANES * g + LANES] for g in range(groups)] for kind in kinds]
     store(pieces, stats)
 
@@ -348,18 +347,17 @@
 
 
 def merge(kept, received, groups):
-    sums_a, (high_a, low_a, *total_a) = unpack(kept, groups)
-    sums_b, (high_b, low_b, *total_b) = unpack(received, groups)
-    larger = high_a + low_a >= high_b + low_b
-    high = jnp.where(larger, high_a, high_b)
-    low = jnp.where(larger, low_a, low_b)
-    scale_a = jnp.exp(high_a + low_a - (high + low))
-    scale_b = jnp.exp(high_b + low_b - (high + low))
+    sums_a, (max_a, total_a, *_) = unpack(kept, groups)
+    sums_b, (max_b, total_b, *_) = unpack(received, groups)
+    local_max = jnp.maximum(max_a, max_b)
+    scale_a = jnp.exp(max_a - local_max)
+    scale_b = jnp.exp(max_b - local_max)
     sums = sums_a * scale_a[..., None, :] + sums_b * scale_b[..., None, :]
-    total = (total_a[0] + total_a[1]) * scale_a + (total_b[0] + total_b[1]) * scale_b
-    total_high = lax.reduce_precision(total, 8, 7)
-    lead = kept.shape[:-2]
-    return [sums.reshape(*lead, OWN * groups, LANES), high, low, total_high, total - total_high]
+    excess = total_a * scale_a + total_b * scale_b - 1.0
+    high = lax.reduce_precision(local_max, 8, 7)
+    middle = lax.reduce_precision(local_max - high, 8, 7)
+    low = local_max - high - middle
+    return [sums.reshape(*kept.shape[:-2], OWN * groups, LANES), high, middle, low, excess]
 
 
 def per_device(hidden_states, head_weight, sign_bits, bucket_ids):
@@ -372,14 +370,13 @@
     table = jnp.where(buckets == bucket_ids[None, :], 2 * sign_bits[None, :] - 1, 0).astype(jnp.bfloat16)
 
     part_a, part_b = place(place_first_kernel, around(hidden_states.T, Y), (SIDE, features, half))
-    own = place(place_second_kernel, around(part_a, X) + around(part_b, Z), (SIDE, SIDE, features, half))
+    own = place(place_second_kernel, around_by_ring(part_a, X) + around_by_ring(part_b, Z), (SIDE, SIDE, features, half))
     near = [ring(p, a) for p, a in zip(own, (Z, X))]
     other = [swap(p) for p in own]
     message_a = whole_blocks(weights, table, ("own",), (own[0], other[0]), ())
     other, message_a = lax.optimization_barrier((other, message_a))
     near_other = [ring(p, a) for p, a in zip(other, (Z, X))]
     near = lax.optimization_barrier(near)
-    near_other = lax.optimization_barrier(near_other)
     far = [ring(p, a) for p, a in zip(near, (Z, X))]
     back = [swap(p) for p in near]
     back_other = [swap(p) for p in near_other]
@@ -396,10 +393,10 @@
     teams = [[device_at(x, y, z, c) for x in range(SIDE) for y in range(SIDE) for z in range(SIDE)] for c in range(CORES)]
     packed = packed.reshape(PLANE * SIDE, packed.shape[2], LANES)
     received = lax.all_to_all(packed, BOTH, 0, 0, axis_index_groups=teams, tiled=True).astype(jnp.float32)
-    sums, (high, low, *totals) = unpack(received.reshape(PLANE * SIDE, 2, -1, LANES), groups)
-    local_max = high + low
+    sums, (high, middle, low, excess) = unpack(received.reshape(PLANE * SIDE, 2, -1, LANES), groups)
+    local_max = high + middle + low
     rescale = jnp.exp(local_max - jnp.max(local_max, axis=0))
-    row_total = jnp.sum((totals[0] + totals[1]) * rescale, axis=0)
+    row_total = jnp.sum((1.0 + excess) * rescale, axis=0)
     bucket_sums = jnp.sum(sums * rescale[..., None, :], axis=0)
     factor = jnp.sqrt(jnp.float32(V) * jnp.float32(B))
     sketch = bucket_sums / row_total[..., None, :] * factor

time: 164 us -> 159 us (0.970)
  waiting for transfers between devices: 55.5 us -> 52.8 us
    ppermute x25, waiting for transfers between devices: 55.5 us -> 52.8 us  [permute(): return lax.ppermute(array, BOTH, pairs)]
  transfers between devices with their start and end apart: 25 -> 25, of which waited for: 17 -> 17; matrix products, arithmetic and copies ran while one was open for 0% -> 0% of each run, Pallas kernels for 11% -> 12%
where the time goes in v3:
time: 159 us
  waiting for transfers between devices  52.8 us (33%)
  Pallas kernels  45.8 us (29%)
  blocking collectives  28.5 us (18%)
  starting transfers between devices  24 us (15%)
  local copies, waits for them, and re-layouts  4.51 us (3%)
  other arithmetic  2.5 us (2%)
    ppermute x25, waiting for transfers between devices, permute(): return lax.ppermute(array, BOTH, pairs)  52.8 us
    all_to_all x1, blocking collectives, per_device(): lax.all_to_all(packed, BOTH, 0, 0, axis_index_groups=teams, tiled=True)  28.5 us
    pallas_call x1, Pallas kernels, finish(): pl.pallas_call(finish_kernel, grid=(3,), in_specs=[ANY, pl.BlockSpec(tabl...  25.7 us
    ppermute x25, starting transfers between devices, permute(): return lax.ppermute(array, BOTH, pairs)  24 us
    pallas_call x2, Pallas kernels, whole_blocks(): pl.pallas_call(functools.partial(whole_kernel, which=which), grid=(steps,...  19.1 us
  transfers between devices with their start and end apart: 25, of which 17 were waited for; matrix products, arithmetic and copies ran while one was open for 0% of the time, Pallas kernels for 12%

profile of v3, /device:TPU:0, one launch (start us, length us, event | category | flops | bytes accessed | tf_op | source)
XLA Modules:
  0.0 159.1 jit_solution(2534215801641313011)
XLA Ops:
  0.6 3.4 %collective-permute-start.2 = (bf16[160,512]{1,0:T(8,128)(2,1)}, bf16[160,512]{1,0:T(8,128)(2,1)S(1)}, u32[]{:S(2)}, u32[]{:S(2)}) collective-permute-start(bf16[160,512]{1,0:T(8,128)(2,1)} %bitcast.85), channel_id=1, source_target_pairs={{0,16},{1,17},{2,18},{3,19},{4,20},{5,21},{6,22},{7,23},{8,24},{9,... | collective-permute-start | bytes 491528 | tf_op jit(solution)/shard_map/ppermute | solution.py:39
  4.0 1.1 collective-permute-start.1
  5.0 1.0 collective-permute-start
  6.0 3.5 %collective-permute-done.2.far = bf16[160,512]{1,0:T(8,128)(2,1)S(1)} collective-permute-done((bf16[160,512]{1,0:T(8,128)(2,1)}, bf16[160,512]{1,0:T(8,128)(2,1)S(1)}, u32[]{:S(2)}, u32[]{:S(2)}) %collective-permute-start.2) | collective-permute-done | bytes 163872 | tf_op jit(solution)/shard_map/ppermute | solution.py:39
  9.5 2.8 %collective-permute-done.1.upper = bf16[160,512]{1,0:T(8,128)(2,1)S(1)} collective-permute-done((bf16[160,512]{1,0:T(8,128)(2,1)}, bf16[160,512]{1,0:T(8,128)(2,1)S(1)}, u32[]{:S(2)}, u32[]{:S(2)}) %collective-permute-start.1) | collective-permute-done | bytes 163872 | tf_op jit(solution)/shard_map/ppermute | solution.py:39
  12.3 0.1 collective-permute-done.lower
  12.4 0.9 copy-done
  13.3 0.1 shard_map.59
  13.5 1.6 %collective-permute-start.3 = (bf16[4,160,256]{2,1,0:T(8,128)(2,1)S(1)}, bf16[4,160,256]{2,1,0:T(8,128)(2,1)S(1)}, u32[]{:S(2)}, u32[]{:S(2)}) collective-permute-start(bf16[4,160,256]{2,1,0:T(8,128)(2,1)S(1)} %get-tuple-element.26.refs_0_), channel_id=1, source_target_pairs={{0,32},{1,33},{2,34},{3,35},{4,100},{5,101},{6,102},{7,103},{8,40}... | collective-permute-start | bytes 983048 | tf_op jit(solution)/shard_map/ppermute | solution.py:39
  15.1 1.9 %collective-permute-start.6 = (bf16[4,160,256]{2,1,0:T(8,128)(2,1)S(1)}, bf16[4,160,256]{2,1,0:T(8,128)(2,1)S(1)}, u32[]{:S(2)}, u32[]{:S(2)}) collective-permute-start(bf16[4,160,256]{2,1,0:T(8,128)(2,1)S(1)} %get-tuple-element.27.refs_4_), channel_id=1, source_target_pairs={{0,1},{1,2},{2,3},{3,0},{4,7},{5,4},{6,5},{7,6},{8,9},{9,10},{10,1... | collective-permute-start | bytes 983048 | tf_op jit(solution)/shard_map/ppermute | solution.py:39
  17.0 1.7 %collective-permute-start.4 = (bf16[4,160,256]{2,1,0:T(8,128)(2,1)S(1)}, bf16[4,160,256]{2,1,0:T(8,128)(2,1)S(1)}, u32[]{:S(2)}, u32[]{:S(2)}) collective-permute-start(bf16[4,160,256]{2,1,0:T(8,128)(2,1)S(1)} %get-tuple-element.26.refs_0_), channel_id=1, source_target_pairs={{0,96},{1,97},{2,98},{3,99},{4,36},{5,37},{6,38},{7,39},{8,104},{9... | collective-permute-start | bytes 983048 | tf_op jit(solution)/shard_map/ppermute | solution.py:39
  18.8 2.1 %collective-permute-start.7 = (bf16[4,160,256]{2,1,0:T(8,128)(2,1)S(1)}, bf16[4,160,256]{2,1,0:T(8,128)(2,1)S(1)}, u32[]{:S(2)}, u32[]{:S(2)}) collective-permute-start(bf16[4,160,256]{2,1,0:T(8,128)(2,1)S(1)} %get-tuple-element.27.refs_4_), channel_id=1, source_target_pairs={{0,3},{1,0},{2,1},{3,2},{4,5},{5,6},{6,7},{7,4},{8,11},{9,8},{10,9... | collective-permute-start | bytes 983048 | tf_op jit(solution)/shard_map/ppermute | solution.py:39
  20.9 1.0 collective-permute-done.3.refs_1_
  21.9 0.7 collective-permute-start.5
  22.6 3.1 %collective-permute-done.6.refs_5_ = bf16[4,160,256]{2,1,0:T(8,128)(2,1)S(1)} collective-permute-done((bf16[4,160,256]{2,1,0:T(8,128)(2,1)S(1)}, bf16[4,160,256]{2,1,0:T(8,128)(2,1)S(1)}, u32[]{:S(2)}, u32[]{:S(2)}) %collective-permute-start.6) | collective-permute-done | bytes 327712 | tf_op jit(solution)/shard_map/ppermute | solution.py:39
  25.7 1.2 collective-permute-start.8
  26.9 0.0 collective-permute-done.4.refs_2_
  26.9 0.0 collective-permute-done.7.refs_6_
  26.9 3.2 %collective-permute-done.5.refs_3_ = bf16[4,160,256]{2,1,0:T(8,128)(2,1)S(1)} collective-permute-done((bf16[4,160,256]{2,1,0:T(8,128)(2,1)S(1)}, bf16[4,160,256]{2,1,0:T(8,128)(2,1)S(1)}, u32[]{:S(2)}, u32[]{:S(2)}) %collective-permute-start.5) | collective-permute-done | bytes 327712 | tf_op jit(solution)/shard_map/ppermute | solution.py:39
  30.1 4.1 %collective-permute-done.8.refs_7_ = bf16[4,160,256]{2,1,0:T(8,128)(2,1)S(1)} collective-permute-done((bf16[4,160,256]{2,1,0:T(8,128)(2,1)S(1)}, bf16[4,160,256]{2,1,0:T(8,128)(2,1)S(1)}, u32[]{:S(2)}, u32[]{:S(2)}) %collective-permute-start.8) | collective-permute-done | bytes 327712 | tf_op jit(solution)/shard_map/ppermute | solution.py:39
  34.2 0.9 shard_map.60
  35.1 0.1 collective-permute-start.15
  35.2 0.5 collective-permute-start.16
  35.7 1.0 collective-permute-start.9
  36.7 1.4 collective-permute-start.10
  38.2 0.4 select_convert_fusion.table_ref
  38.6 7.8 %shard_map.61 = (f32[16,4,40,128]{3,2,1,0:T(8,128)S(1)}, f32[16,4,40,128]{3,2,1,0:T(8,128)S(1)}) custom-call(bf16[1187,5120]{1,0:T(8,128)(2,1)} %bitcast.89, bf16[512,1187]{1,0:T(8,128)(2,1)S(1)} %select_convert_fusion.table_ref, bf16[4,4,160,256]{3,2,1,0:T(8,128)(2,1)S(1)} %get-tuple-element.28.refs_0_, ...), custom_call_target="tpu_custom_call" | custom-call | flops 3422814208 | bytes 14776320 | tf_op jit(solution)/shard_map/pallas_call | solution.py:205
  46.4 0.0 collective-permute-done.16.refs_3_
  46.5 0.7 collective-permute-start.17
  47.2 7.4 %collective-permute-done.9.refs_0_ = bf16[4,4,160,256]{3,2,1,0:T(8,128)(2,1)S(1)} collective-permute-done((bf16[4,4,160,256]{3,2,1,0:T(8,128)(2,1)S(1)}, bf16[4,4,160,256]{3,2,1,0:T(8,128)(2,1)S(1)}, u32[]{:S(2)}, u32[]{:S(2)}) %collective-permute-start.9) | collective-permute-done | bytes 1310752 | tf_op jit(solution)/shard_map/ppermute | solution.py:39
  54.5 1.0 collective-permute-done.10.refs_4_
  55.5 1.4 collective-permute-start.19
  57.0 11.6 %collective-permute-done.17.refs_1_ = bf16[4,4,160,256]{3,2,1,0:T(8,128)(2,1)S(1)} collective-permute-done((bf16[4,4,160,256]{3,2,1,0:T(8,128)(2,1)S(1)}, bf16[4,4,160,256]{3,2,1,0:T(8,128)(2,1)S(1)}, u32[]{:S(2)}, u32[]{:S(2)}) %collective-permute-start.17) | collective-permute-done | bytes 1310752 | tf_op jit(solution)/shard_map/ppermute | solution.py:39
  68.6 2.0 %collective-permute-start.14 = (bf16[4,4,160,256]{3,2,1,0:T(8,128)(2,1)S(1)}, bf16[4,4,160,256]{3,2,1,0:T(8,128)(2,1)S(1)}, u32[]{:S(2)}, u32[]{:S(2)}) collective-permute-start(bf16[4,4,160,256]{3,2,1,0:T(8,128)(2,1)S(1)} %collective-permute-done.10.refs_4_), channel_id=1, source_target_pairs={{0,4},{1,5},{2,6},{3,7},{4,0},{5,1},{6,2},{7,3},{8,12},{9,13},{10,... | collective-permute-start | bytes 3932168 | tf_op jit(solution)/shard_map/ppermute | solution.py:39
  70.6 0.9 collective-permute-start.12
  71.5 2.9 %collective-permute-done.19.refs_5_ = bf16[4,4,160,256]{3,2,1,0:T(8,128)(2,1)S(1)} collective-permute-done((bf16[4,4,160,256]{3,2,1,0:T(8,128)(2,1)S(1)}, bf16[4,4,160,256]{3,2,1,0:T(8,128)(2,1)S(1)}, u32[]{:S(2)}, u32[]{:S(2)}) %collective-permute-start.19) | collective-permute-done | bytes 1310752 | tf_op jit(solution)/shard_map/ppermute | solution.py:39
  74.4 0.0 collective-permute-start.20
  74.4 11.2 %shard_map.62 = (f32[16,4,40,128]{3,2,1,0:T(8,128)S(1)}, f32[16,4,40,128]{3,2,1,0:T(8,128)S(1)}) custom-call(bf16[1187,5120]{1,0:T(8,128)(2,1)} %bitcast.90, bf16[512,1187]{1,0:T(8,128)(2,1)S(1)} %select_convert_fusion.table_ref, bf16[4,4,160,256]{3,2,1,0:T(8,128)(2,1)S(1)} %collective-permute-done.9.refs_0_, ...), custom_call_target="tpu_custom_call", output_to_operand_aliasing={{0}: (6, {}), {1}: (7, {})} | custom-call | flops 6845628416 | bytes 17397760 | tf_op jit(solution)/shard_map/pallas_call | solution.py:205
  85.6 1.8 %collective-permute-done.11.refs_0_ = bf16[4,4,160,256]{3,2,1,0:T(8,128)(2,1)S(1)} collective-permute-done((bf16[4,4,160,256]{3,2,1,0:T(8,128)(2,1)S(1)}, bf16[4,4,160,256]{3,2,1,0:T(8,128)(2,1)S(1)}, u32[]{:S(2)}, u32[]{:S(2)}) %collective-permute-start.11) | collective-permute-done | bytes 1310752 | tf_op jit(solution)/shard_map/ppermute | solution.py:39
  87.4 2.0 %collective-permute-done.12.refs_8_ = bf16[4,4,160,256]{3,2,1,0:T(8,128)(2,1)S(1)} collective-permute-done((bf16[4,4,160,256]{3,2,1,0:T(8,128)(2,1)S(1)}, bf16[4,4,160,256]{3,2,1,0:T(8,128)(2,1)S(1)}, u32[]{:S(2)}, u32[]{:S(2)}) %collective-permute-start.12) | collective-permute-done | bytes 1310752 | tf_op jit(solution)/shard_map/ppermute | solution.py:39
  89.4 0.1 collective-permute-start.21
  89.5 0.5 collective-permute-start.22
  90.0 2.5 %collective-permute-done.21.refs_1_ = bf16[4,4,160,256]{3,2,1,0:T(8,128)(2,1)S(1)} collective-permute-done((bf16[4,4,160,256]{3,2,1,0:T(8,128)(2,1)S(1)}, bf16[4,4,160,256]{3,2,1,0:T(8,128)(2,1)S(1)}, u32[]{:S(2)}, u32[]{:S(2)}) %collective-permute-start.21) | collective-permute-done | bytes 1310752 | tf_op jit(solution)/shard_map/ppermute | solution.py:39
  92.5 1.9 %collective-permute-done.22.refs_9_ = bf16[4,4,160,256]{3,2,1,0:T(8,128)(2,1)S(1)} collective-permute-done((bf16[4,4,160,256]{3,2,1,0:T(8,128)(2,1)S(1)}, bf16[4,4,160,256]{3,2,1,0:T(8,128)(2,1)S(1)}, u32[]{:S(2)}, u32[]{:S(2)}) %collective-permute-start.22) | collective-permute-done | bytes 1310752 | tf_op jit(solution)/shard_map/ppermute | solution.py:39
  94.4 1.1 copy-done.10
  95.5 25.7 %shard_map.63 = (f32[16,4,40,128]{3,2,1,0:T(8,128)S(1)}, f32[16,4,40,128]{3,2,1,0:T(8,128)S(1)}, f32[16,4,40,128]{3,2,1,0:T(8,128)S(1)}, f32[16,4,40,128]{3,2,1,0:T(8,128)S(1)}) custom-call(bf16[1187,5120]{1,0:T(8,128)(2,1)} %bitcast.91, bf16[512,1187]{1,0:T(8,128)(2,1)S(1)} %select_convert_fusion.table_ref, ...), custom_call_target="tpu_custom_call", output_to_operand_aliasing={{0}: (12, {}), {1}: (13, {})} | custom-call | flops 17114071040 | bytes 25262080 | tf_op jit(solution)/shard_map/pallas_call | solution.py:315
  121.2 0.2 collective-permute-start.23
  121.4 0.4 collective-permute-start.24
  122.0 2.3 %collective-permute-done.23 = f32[16,4,40,128]{3,2,1,0:T(8,128)S(1)} collective-permute-done((f32[16,4,40,128]{3,2,1,0:T(8,128)S(1)}, f32[16,4,40,128]{3,2,1,0:T(8,128)S(1)}, u32[]{:S(2)}, u32[]{:S(2)}) %collective-permute-start.23) | collective-permute-done | bytes 1310752 | tf_op jit(solution)/shard_map/ppermute | solution.py:39
  124.4 0.1 fusion.11
  124.5 1.7 %collective-permute-done.24 = f32[16,4,40,128]{3,2,1,0:T(8,128)S(1)} collective-permute-done((f32[16,4,40,128]{3,2,1,0:T(8,128)S(1)}, f32[16,4,40,128]{3,2,1,0:T(8,128)S(1)}, u32[]{:S(2)}, u32[]{:S(2)}) %collective-permute-start.24) | collective-permute-done | bytes 1310752 | tf_op jit(solution)/shard_map/ppermute | solution.py:39
  126.2 0.1 fusion.13
  126.4 0.1 add_convert_fusion.1
  126.7 0.1 add_convert_fusion
  127.0 0.2 fusion.4
  127.3 0.2 fusion.2
  127.5 1.0 concatenate.11
  128.5 28.5 %all_to_all.5 = f16[64,80,128]{2,1,0:T(8,128)(2,1)S(1)} all-to-all(f16[64,80,128]{2,1,0:T(8,128)(2,1)S(1)} %concatenate.11), channel_id=1, replica_groups={{0,1,2,3,8,9,10,11,16,17,18,19,24,25,26,27,32,33,34,35,40,41,42,43,48,4..., dimensions={0} | all-to-all | bytes 2621440 | tf_op jit(solution)/shard_map/all_to_all | solution.py:395
  157.0 0.2 convert.43
  157.2 0.1 fusion.18
  157.4 0.1 fusion.10
  157.5 0.3 fusion
  157.8 0.6 log_negate_fusion
  158.4 0.6 reshape.161
  (56 shorter events, 0.9 us)
Async XLA Ops:
  0.6 8.9 %collective-permute-start.2 = (bf16[160,512]{1,0:T(8,128)(2,1)}, bf16[160,512]{1,0:T(8,128)(2,1)S(1)}, u32[]{:S(2)}, u32[]{:S(2)}) collective-permute-start(bf16[160,512]{1,0:T(8,128)(2,1)} %bitcast.85), channel_id=1, source_target_pairs={{0,16},{1,17},{2,18},{3,19},{4,20},{5,21},{6,22},{7,23},{8,24},{9,... | collective-permute-start | bytes 491528 | tf_op jit(solution)/shard_map/ppermute | solution.py:39
  4.0 8.3 %collective-permute-start.1 = (bf16[160,512]{1,0:T(8,128)(2,1)}, bf16[160,512]{1,0:T(8,128)(2,1)S(1)}, u32[]{:S(2)}, u32[]{:S(2)}) collective-permute-start(bf16[160,512]{1,0:T(8,128)(2,1)} %bitcast.86), channel_id=1, source_target_pairs={{0,24},{1,25},{2,26},{3,27},{4,28},{5,29},{6,30},{7,31},{8,0},{9,1... | collective-permute-start | bytes 491528 | tf_op jit(solution)/shard_map/ppermute | solution.py:39
  5.0 7.4 %collective-permute-start = (bf16[160,512]{1,0:T(8,128)(2,1)}, bf16[160,512]{1,0:T(8,128)(2,1)S(1)}, u32[]{:S(2)}, u32[]{:S(2)}) collective-permute-start(bf16[160,512]{1,0:T(8,128)(2,1)} %bitcast.87), channel_id=1, source_target_pairs={{0,8},{1,9},{2,10},{3,11},{4,12},{5,13},{6,14},{7,15},{8,16},{9,17... | collective-permute-start | bytes 491528 | tf_op jit(solution)/shard_map/ppermute | solution.py:39
  12.4 0.9 copy-start
  13.5 8.4 %collective-permute-start.3 = (bf16[4,160,256]{2,1,0:T(8,128)(2,1)S(1)}, bf16[4,160,256]{2,1,0:T(8,128)(2,1)S(1)}, u32[]{:S(2)}, u32[]{:S(2)}) collective-permute-start(bf16[4,160,256]{2,1,0:T(8,128)(2,1)S(1)} %get-tuple-element.26.refs_0_), channel_id=1, source_target_pairs={{0,32},{1,33},{2,34},{3,35},{4,100},{5,101},{6,102},{7,103},{8,40}... | collective-permute-start | bytes 983048 | tf_op jit(solution)/shard_map/ppermute | solution.py:39
  15.1 20.6 %copy-start.2 = (s32[1187]{0:T(1024)S(1)}, s32[1187]{0:T(1024)}, u32[]{:S(2)}) copy-start(s32[1187]{0:T(1024)} %param.6) | copy-start | bytes 14248
  15.1 23.1 %copy-start.3 = (s32[1187]{0:T(1024)S(1)}, s32[1187]{0:T(1024)}, u32[]{:S(2)}) copy-start(s32[1187]{0:T(1024)} %param.7) | copy-start | bytes 14248
  15.1 10.6 %collective-permute-start.6 = (bf16[4,160,256]{2,1,0:T(8,128)(2,1)S(1)}, bf16[4,160,256]{2,1,0:T(8,128)(2,1)S(1)}, u32[]{:S(2)}, u32[]{:S(2)}) collective-permute-start(bf16[4,160,256]{2,1,0:T(8,128)(2,1)S(1)} %get-tuple-element.27.refs_4_), channel_id=1, source_target_pairs={{0,1},{1,2},{2,3},{3,0},{4,7},{5,4},{6,5},{7,6},{8,9},{9,10},{10,1... | collective-permute-start | bytes 983048 | tf_op jit(solution)/shard_map/ppermute | solution.py:39
  17.0 9.9 %collective-permute-start.4 = (bf16[4,160,256]{2,1,0:T(8,128)(2,1)S(1)}, bf16[4,160,256]{2,1,0:T(8,128)(2,1)S(1)}, u32[]{:S(2)}, u32[]{:S(2)}) collective-permute-start(bf16[4,160,256]{2,1,0:T(8,128)(2,1)S(1)} %get-tuple-element.26.refs_0_), channel_id=1, source_target_pairs={{0,96},{1,97},{2,98},{3,99},{4,36},{5,37},{6,38},{7,39},{8,104},{9... | collective-permute-start | bytes 983048 | tf_op jit(solution)/shard_map/ppermute | solution.py:39
  18.8 8.1 %collective-permute-start.7 = (bf16[4,160,256]{2,1,0:T(8,128)(2,1)S(1)}, bf16[4,160,256]{2,1,0:T(8,128)(2,1)S(1)}, u32[]{:S(2)}, u32[]{:S(2)}) collective-permute-start(bf16[4,160,256]{2,1,0:T(8,128)(2,1)S(1)} %get-tuple-element.27.refs_4_), channel_id=1, source_target_pairs={{0,3},{1,0},{2,1},{3,2},{4,5},{5,6},{6,7},{7,4},{8,11},{9,8},{10,9... | collective-permute-start | bytes 983048 | tf_op jit(solution)/shard_map/ppermute | solution.py:39
  21.9 8.3 %collective-permute-start.5 = (bf16[4,160,256]{2,1,0:T(8,128)(2,1)S(1)}, bf16[4,160,256]{2,1,0:T(8,128)(2,1)S(1)}, u32[]{:S(2)}, u32[]{:S(2)}) collective-permute-start(bf16[4,160,256]{2,1,0:T(8,128)(2,1)S(1)} %collective-permute-done.3.refs_1_), channel_id=1, source_target_pairs={{0,32},{1,33},{2,34},{3,35},{4,100},{5,101},{6,102},{7,103},{8,40}... | collective-permute-start | bytes 983048 | tf_op jit(solution)/shard_map/ppermute | solution.py:39
  25.7 8.5 %collective-permute-start.8 = (bf16[4,160,256]{2,1,0:T(8,128)(2,1)S(1)}, bf16[4,160,256]{2,1,0:T(8,128)(2,1)S(1)}, u32[]{:S(2)}, u32[]{:S(2)}) collective-permute-start(bf16[4,160,256]{2,1,0:T(8,128)(2,1)S(1)} %collective-permute-done.6.refs_5_), channel_id=1, source_target_pairs={{0,1},{1,2},{2,3},{3,0},{4,7},{5,4},{6,5},{7,6},{8,9},{9,10},{10,1... | collective-permute-start | bytes 983048 | tf_op jit(solution)/shard_map/ppermute | solution.py:39
  35.1 11.3 %copy-start.1 = (bf16[4,4,160,256]{3,2,1,0:T(8,128)(2,1)}, bf16[4,4,160,256]{3,2,1,0:T(8,128)(2,1)S(1)}, u32[]{:S(2)}) copy-start(bf16[4,4,160,256]{3,2,1,0:T(8,128)(2,1)S(1)} %get-tuple-element.29.refs_2_) | copy-start | bytes 3932164
  35.1 3.4 %collective-permute-start.15 = (bf16[4,4,160,256]{3,2,1,0:T(8,128)(2,1)S(1)}, bf16[4,4,160,256]{3,2,1,0:T(8,128)(2,1)S(1)}, u32[]{:S(2)}, u32[]{:S(2)}) collective-permute-start(bf16[4,4,160,256]{3,2,1,0:T(8,128)(2,1)S(1)} %get-tuple-element.28.refs_0_), channel_id=1, source_target_pairs={{0,4},{1,5},{2,6},{3,7},{4,0},{5,1},{6,2},{7,3},{8,12},{9,13},{10,... | collective-permute-start | bytes 3932168 | tf_op jit(solution)/shard_map/ppermute | solution.py:39
  35.2 11.2 %collective-permute-start.16 = (bf16[4,4,160,256]{3,2,1,0:T(8,128)(2,1)S(1)}, bf16[4,4,160,256]{3,2,1,0:T(8,128)(2,1)S(1)}, u32[]{:S(2)}, u32[]{:S(2)}) collective-permute-start(bf16[4,4,160,256]{3,2,1,0:T(8,128)(2,1)S(1)} %get-tuple-element.29.refs_2_), channel_id=1, source_target_pairs={{0,4},{1,5},{2,6},{3,7},{4,0},{5,1},{6,2},{7,3},{8,12},{9,13},{10,... | collective-permute-start | bytes 3932168 | tf_op jit(solution)/shard_map/ppermute | solution.py:39
  35.7 18.8 %collective-permute-start.9 = (bf16[4,4,160,256]{3,2,1,0:T(8,128)(2,1)S(1)}, bf16[4,4,160,256]{3,2,1,0:T(8,128)(2,1)S(1)}, u32[]{:S(2)}, u32[]{:S(2)}) collective-permute-start(bf16[4,4,160,256]{3,2,1,0:T(8,128)(2,1)S(1)} %get-tuple-element.28.refs_0_), channel_id=1, source_target_pairs={{0,1},{1,2},{2,3},{3,0},{4,7},{5,4},{6,5},{7,6},{8,9},{9,10},{10,1... | collective-permute-start | bytes 3932168 | tf_op jit(solution)/shard_map/ppermute | solution.py:39
  36.7 18.8 %collective-permute-start.10 = (bf16[4,4,160,256]{3,2,1,0:T(8,128)(2,1)S(1)}, bf16[4,4,160,256]{3,2,1,0:T(8,128)(2,1)S(1)}, u32[]{:S(2)}, u32[]{:S(2)}) collective-permute-start(bf16[4,4,160,256]{3,2,1,0:T(8,128)(2,1)S(1)} %get-tuple-element.29.refs_2_), channel_id=1, source_target_pairs={{0,32},{1,33},{2,34},{3,35},{4,100},{5,101},{6,102},{7,103},{8,40}... | collective-permute-start | bytes 3932168 | tf_op jit(solution)/shard_map/ppermute | solution.py:39
  46.5 39.2 %copy-start.4 = (bf16[4,4,160,256]{3,2,1,0:T(8,128)(2,1)}, bf16[4,4,160,256]{3,2,1,0:T(8,128)(2,1)S(1)}, u32[]{:S(2)}) copy-start(bf16[4,4,160,256]{3,2,1,0:T(8,128)(2,1)S(1)} %collective-permute-done.16.refs_3_) | copy-start | bytes 3932164
  46.5 22.1 %collective-permute-start.17 = (bf16[4,4,160,256]{3,2,1,0:T(8,128)(2,1)S(1)}, bf16[4,4,160,256]{3,2,1,0:T(8,128)(2,1)S(1)}, u32[]{:S(2)}, u32[]{:S(2)}) collective-permute-start(bf16[4,4,160,256]{3,2,1,0:T(8,128)(2,1)S(1)} %collective-permute-done.15.refs_1_), channel_id=1, source_target_pairs={{0,1},{1,2},{2,3},{3,0},{4,7},{5,4},{6,5},{7,6},{8,9},{9,10},{10,1... | collective-permute-start | bytes 3932168 | tf_op jit(solution)/shard_map/ppermute | solution.py:39
  55.5 30.1 %copy-start.5 = (bf16[4,4,160,256]{3,2,1,0:T(8,128)(2,1)}, bf16[4,4,160,256]{3,2,1,0:T(8,128)(2,1)S(1)}, u32[]{:S(2)}) copy-start(bf16[4,4,160,256]{3,2,1,0:T(8,128)(2,1)S(1)} %collective-permute-done.10.refs_4_) | copy-start | bytes 3932164
  55.5 15.0 %collective-permute-start.13 = (bf16[4,4,160,256]{3,2,1,0:T(8,128)(2,1)S(1)}, bf16[4,4,160,256]{3,2,1,0:T(8,128)(2,1)S(1)}, u32[]{:S(2)}, u32[]{:S(2)}) collective-permute-start(bf16[4,4,160,256]{3,2,1,0:T(8,128)(2,1)S(1)} %collective-permute-done.9.refs_0_), channel_id=1, source_target_pairs={{0,4},{1,5},{2,6},{3,7},{4,0},{5,1},{6,2},{7,3},{8,12},{9,13},{10,... | collective-permute-start | bytes 3932168 | tf_op jit(solution)/shard_map/ppermute | solution.py:39
  55.5 18.8 %collective-permute-start.19 = (bf16[4,4,160,256]{3,2,1,0:T(8,128)(2,1)S(1)}, bf16[4,4,160,256]{3,2,1,0:T(8,128)(2,1)S(1)}, u32[]{:S(2)}, u32[]{:S(2)}) collective-permute-start(bf16[4,4,160,256]{3,2,1,0:T(8,128)(2,1)S(1)} %collective-permute-done.16.refs_3_), channel_id=1, source_target_pairs={{0,32},{1,33},{2,34},{3,35},{4,100},{5,101},{6,102},{7,103},{8,40}... | collective-permute-start | bytes 3932168 | tf_op jit(solution)/shard_map/ppermute | solution.py:39
  68.6 5.8 %collective-permute-start.18 = (bf16[4,4,160,256]{3,2,1,0:T(8,128)(2,1)S(1)}, bf16[4,4,160,256]{3,2,1,0:T(8,128)(2,1)S(1)}, u32[]{:S(2)}, u32[]{:S(2)}) collective-permute-start(bf16[4,4,160,256]{3,2,1,0:T(8,128)(2,1)S(1)} %collective-permute-done.17.refs_1_), channel_id=1, source_target_pairs={{0,4},{1,5},{2,6},{3,7},{4,0},{5,1},{6,2},{7,3},{8,12},{9,13},{10,... | collective-permute-start | bytes 3932168 | tf_op jit(solution)/shard_map/ppermute | solution.py:39
  68.6 18.8 %collective-permute-start.11 = (bf16[4,4,160,256]{3,2,1,0:T(8,128)(2,1)S(1)}, bf16[4,4,160,256]{3,2,1,0:T(8,128)(2,1)S(1)}, u32[]{:S(2)}, u32[]{:S(2)}) collective-permute-start(bf16[4,4,160,256]{3,2,1,0:T(8,128)(2,1)S(1)} %collective-permute-done.9.refs_0_), channel_id=1, source_target_pairs={{0,1},{1,2},{2,3},{3,0},{4,7},{5,4},{6,5},{7,6},{8,9},{9,10},{10,1... | collective-permute-start | bytes 3932168 | tf_op jit(solution)/shard_map/ppermute | solution.py:39
  68.6 18.8 %collective-permute-start.14 = (bf16[4,4,160,256]{3,2,1,0:T(8,128)(2,1)S(1)}, bf16[4,4,160,256]{3,2,1,0:T(8,128)(2,1)S(1)}, u32[]{:S(2)}, u32[]{:S(2)}) collective-permute-start(bf16[4,4,160,256]{3,2,1,0:T(8,128)(2,1)S(1)} %collective-permute-done.10.refs_4_), channel_id=1, source_target_pairs={{0,4},{1,5},{2,6},{3,7},{4,0},{5,1},{6,2},{7,3},{8,12},{9,13},{10,... | collective-permute-start | bytes 3932168 | tf_op jit(solution)/shard_map/ppermute | solution.py:39
  70.6 18.8 %collective-permute-start.12 = (bf16[4,4,160,256]{3,2,1,0:T(8,128)(2,1)S(1)}, bf16[4,4,160,256]{3,2,1,0:T(8,128)(2,1)S(1)}, u32[]{:S(2)}, u32[]{:S(2)}) collective-permute-start(bf16[4,4,160,256]{3,2,1,0:T(8,128)(2,1)S(1)} %collective-permute-done.10.refs_4_), channel_id=1, source_target_pairs={{0,32},{1,33},{2,34},{3,35},{4,100},{5,101},{6,102},{7,103},{8,40}... | collective-permute-start | bytes 3932168 | tf_op jit(solution)/shard_map/ppermute | solution.py:39
  74.4 11.3 %copy-start.6 = (bf16[4,4,160,256]{3,2,1,0:T(8,128)(2,1)}, bf16[4,4,160,256]{3,2,1,0:T(8,128)(2,1)S(1)}, u32[]{:S(2)}) copy-start(bf16[4,4,160,256]{3,2,1,0:T(8,128)(2,1)S(1)} %collective-permute-done.19.refs_5_) | copy-start | bytes 3932164
  74.4 15.0 %collective-permute-start.20 = (bf16[4,4,160,256]{3,2,1,0:T(8,128)(2,1)S(1)}, bf16[4,4,160,256]{3,2,1,0:T(8,128)(2,1)S(1)}, u32[]{:S(2)}, u32[]{:S(2)}) collective-permute-start(bf16[4,4,160,256]{3,2,1,0:T(8,128)(2,1)S(1)} %collective-permute-done.19.refs_5_), channel_id=1, source_target_pairs={{0,4},{1,5},{2,6},{3,7},{4,0},{5,1},{6,2},{7,3},{8,12},{9,13},{10,... | collective-permute-start | bytes 3932168 | tf_op jit(solution)/shard_map/ppermute | solution.py:39
  87.4 7.0 %copy-start.7 = (bf16[4,4,160,256]{3,2,1,0:T(8,128)(2,1)}, bf16[4,4,160,256]{3,2,1,0:T(8,128)(2,1)S(1)}, u32[]{:S(2)}) copy-start(bf16[4,4,160,256]{3,2,1,0:T(8,128)(2,1)S(1)} %collective-permute-done.14.refs_6_) | copy-start | bytes 3932164
  89.4 5.0 %copy-start.8 = (bf16[4,4,160,256]{3,2,1,0:T(8,128)(2,1)}, bf16[4,4,160,256]{3,2,1,0:T(8,128)(2,1)S(1)}, u32[]{:S(2)}) copy-start(bf16[4,4,160,256]{3,2,1,0:T(8,128)(2,1)S(1)} %collective-permute-done.12.refs_8_) | copy-start | bytes 3932164
  89.4 5.0 %copy-start.9 = (bf16[4,4,160,256]{3,2,1,0:T(8,128)(2,1)}, bf16[4,4,160,256]{3,2,1,0:T(8,128)(2,1)S(1)}, u32[]{:S(2)}) copy-start(bf16[4,4,160,256]{3,2,1,0:T(8,128)(2,1)S(1)} %collective-permute-done.20.refs_7_) | copy-start | bytes 3932164
  89.4 3.1 %collective-permute-start.21 = (bf16[4,4,160,256]{3,2,1,0:T(8,128)(2,1)S(1)}, bf16[4,4,160,256]{3,2,1,0:T(8,128)(2,1)S(1)}, u32[]{:S(2)}, u32[]{:S(2)}) collective-permute-start(bf16[4,4,160,256]{3,2,1,0:T(8,128)(2,1)S(1)} %collective-permute-done.11.refs_0_), channel_id=1, source_target_pairs={{0,4},{1,5},{2,6},{3,7},{4,0},{5,1},{6,2},{7,3},{8,12},{9,13},{10,... | collective-permute-start | bytes 3932168 | tf_op jit(solution)/shard_map/ppermute | solution.py:39
  89.5 4.9 %collective-permute-start.22 = (bf16[4,4,160,256]{3,2,1,0:T(8,128)(2,1)S(1)}, bf16[4,4,160,256]{3,2,1,0:T(8,128)(2,1)S(1)}, u32[]{:S(2)}, u32[]{:S(2)}) collective-permute-start(bf16[4,4,160,256]{3,2,1,0:T(8,128)(2,1)S(1)} %collective-permute-done.12.refs_8_), channel_id=1, source_target_pairs={{0,4},{1,5},{2,6},{3,7},{4,0},{5,1},{6,2},{7,3},{8,12},{9,13},{10,... | collective-permute-start | bytes 3932168 | tf_op jit(solution)/shard_map/ppermute | solution.py:39
  94.4 1.1 copy-start.10
  121.2 3.1 %collective-permute-start.23 = (f32[16,4,40,128]{3,2,1,0:T(8,128)S(1)}, f32[16,4,40,128]{3,2,1,0:T(8,128)S(1)}, u32[]{:S(2)}, u32[]{:S(2)}) collective-permute-start(f32[16,4,40,128]{3,2,1,0:T(8,128)S(1)} %get-tuple-element.47), channel_id=1, source_target_pairs={{0,4},{1,5},{2,6},{3,7},{4,0},{5,1},{6,2},{7,3},{8,12},{9,13},{10,... | collective-permute-start | bytes 3932168 | tf_op jit(solution)/shard_map/ppermute | solution.py:39
  121.4 4.8 %collective-permute-start.24 = (f32[16,4,40,128]{3,2,1,0:T(8,128)S(1)}, f32[16,4,40,128]{3,2,1,0:T(8,128)S(1)}, u32[]{:S(2)}, u32[]{:S(2)}) collective-permute-start(f32[16,4,40,128]{3,2,1,0:T(8,128)S(1)} %get-tuple-element.49), channel_id=1, source_target_pairs={{0,4},{1,5},{2,6},{3,7},{4,0},{5,1},{6,2},{7,3},{8,12},{9,13},{10,... | collective-permute-start | bytes 3932168 | tf_op jit(solution)/shard_map/ppermute | solution.py:39

commit v4 on v3

--- a/solution.py
+++ b/solution.py
@@ -227,11 +227,10 @@
 
 
 def finish_kernel(w_hbm, table_ref, *refs):
-    far_a, part_b, refs = refs[:2], refs[2:10], refs[12:]
-    outs_a, outs_b, refs = refs[:2], refs[2:4], refs[4:]
+    part_b, outs, refs = refs[:8], refs[8:10], refs[10:]
     weights, held, logits, kept, sent, w_sem, x_sem, out_sem = refs
     step = pl.program_id(0)
-    (x, _, z), core = position()
+    (x, _, _), core = position()
     columns = table_ref.shape[1]
     half = held.shape[5] // 2
     groups = half // LANES
@@ -258,85 +257,70 @@
         for k, source in enumerate((kept, sent)):
             pltpu.make_async_copy(source.at[b], outs[k].at[:, block], out_sem.at[b, k]).start()
 
+    def store(pieces, stats):
+        for h in range(2):
+            part = slice(groups * h, groups * h + groups)
+            b = 2 * step + h
+            write((kept.at[b], sent.at[b]), pieces[part], [kind[part] for kind in stats], core)
+            send(b, outs, b)
+
     @pl.when(step == 0)
     def _():
-        for k in range(2):
-            target = held.at[0, :, :, core if k == 0 else 1 - core, :, pl.ds(0, half)]
-            pltpu.make_async_copy(far_a[k], target, x_sem.at[0]).start()
-        for k in range(w_sem.shape[0]):
+        w_copy(0).start()
+        fetch_b(0, 0)
+        for k in range(1, w_sem.shape[0]):
             w_copy(k).start()
-        fetch_b(0, 1)
-        arrived(0, half)
-        tokens = held[0, :, :, :, :, :half].reshape(depth, half)
+        fetch_b(1, 1)
+        arrived(0, 2 * half)
+        tokens = held[0].reshape(depth, 2 * half)
         for k in range(w_sem.shape[0]):
             w_copy(k).wait()
             rows = slice(ROW_BLOCK * k, min(columns, ROW_BLOCK * (k + 1)))
             logits[rows, :] = jnp.dot(weights[rows, :], tokens, preferred_element_type=jnp.float32)
-
-        def store(pieces, stats):
-            write((kept.at[0], sent.at[0]), pieces, stats, core)
-
         summarise(logits[...], table_ref[...], core, store)
-        send(0, outs_a, lax.rem(z + 2, SIDE))
 
     @pl.when(step > 0)
     def _():
-        slot = lax.rem(step, 2)
-
-        @pl.when(step == 1)
-        def _():
-            fetch_b(1, 0)
-
-        arrived(slot, 2 * half)
-        tokens = held[slot].reshape(depth, 2 * half)
+        arrived(1, 2 * half)
+        tokens = held[1].reshape(depth, 2 * half)
         product = jnp.dot(weights[...], tokens, preferred_element_type=jnp.float32)
-
-        def store(pieces, stats):
-            for h in range(2):
-                part = slice(groups * h, groups * h + groups)
-                b = 2 * step - 1 + h
-                write((kept.at[b], sent.at[b]), pieces[part], [kind[part] for kind in stats], core)
-                send(b, outs_b, 2 * step - 2 + h)
-
         summarise(product, table_ref[...], core, store)
 
     @pl.when(step == pl.num_programs(0) - 1)
     def _():
-        for b in range(5):
+        for b in range(SIDE):
             for k, source in enumerate((kept, sent)):
                 pltpu.make_async_copy(source.at[b], source.at[b], out_sem.at[b, k]).wait()
 
 
-def finish(weights, table, far_a, part_b, previous):
+def finish(weights, table, part_b):
     columns, depth = weights.shape
-    features, half = far_a[0].shape[2:]
+    features, half = part_b[0].shape[2:]
     rows = message_rows(half)
     shape = jax.ShapeDtypeStruct((PLANE, SIDE, rows, LANES), jnp.float32)
-    results = pl.pallas_call(
+    return pl.pallas_call(
         finish_kernel,
-        grid=(3,),
-        in_specs=[ANY, pl.BlockSpec(table.shape, lambda i: (0, 0))] + [ANY] * 12,
-        out_specs=[ANY] * 4,
-        out_shape=[shape] * 4,
-        input_output_aliases={12: 0, 13: 1},
+        grid=(2,),
+        in_specs=[ANY, pl.BlockSpec(table.shape, lambda i: (0, 0))] + [ANY] * 8,
+        out_specs=[ANY] * 2,
+        out_shape=[shape] * 2,
         scratch_shapes=[
             pltpu.VMEM((columns, depth), jnp.bfloat16),
             pltpu.VMEM((2, SIDE, SIDE, CORES, features, 2 * half), jnp.bfloat16),
-            pltpu.VMEM((columns, half), jnp.float32),
-            pltpu.VMEM((5, PLANE, rows, LANES), jnp.float32),
-            pltpu.VMEM((5, PLANE, rows, LANES), jnp.float32),
+            pltpu.VMEM((columns, 2 * half), jnp.float32),
+            pltpu.VMEM((SIDE, PLANE, rows, LANES), jnp.float32),
+            pltpu.VMEM((SIDE, PLANE, rows, LANES), jnp.float32),
             pltpu.SemaphoreType.DMA((pl.cdiv(columns, ROW_BLOCK),)),
             pltpu.SemaphoreType.DMA((2,)),
-            pltpu.SemaphoreType.DMA((5, 2)),
+            pltpu.SemaphoreType.DMA((SIDE, 2)),
         ],
         compiler_params=pltpu.CompilerParams(vmem_limit_bytes=VMEM_BYTES),
         cost_estimate=pl.CostEstimate(
-            flops=2 * columns * (depth + B) * 5 * half,
-            bytes_accessed=2 * depth * (columns + 5 * half),
-            transcendentals=columns * 5 * half,
+            flops=2 * columns * (depth + B) * SIDE * half,
+            bytes_accessed=2 * depth * (columns + SIDE * half),
+            transcendentals=columns * SIDE * half,
         ),
-    )(weights, table, *far_a, *part_b, *previous)
-    return results[:2], results[2:]
+    )(weights, table, *part_b)
 
 
 def unpack(message, groups):
@@ -384,7 +368,8 @@
     far, back, back_other, message_a = lax.optimization_barrier((far, back, back_other, message_a))
     far_other = [swap(p) for p in far]
     part_b = (own[1], other[1], near[1], near_other[1], back[1], back_other[1], far[1], far_other[1])
-    message_a, message_b = finish(weights, table, (far[0], far_other[0]), part_b, message_a)
+    message_a = whole_blocks(weights, table, ("far",), (far[0], far_other[0]), message_a)
+    message_b = finish(weights, table, part_b)
 
     pieces = []
     for kept, sent in (message_a, message_b):

time: 159 us -> 160 us (level)
    pallas_call x2 -> x3, Pallas kernels: 19.1 us -> 26.4 us  [whole_blocks(): pl.pallas_call(functools.partial(whole_kernel, which=which), grid=(steps,...]
    pallas_call x1, Pallas kernels: 25.7 us -> 19 us  [finish(): pl.pallas_call(finish_kernel, grid=(2,), in_specs=[ANY, pl.BlockSpec(tabl...]
  transfers between devices with their start and end apart: 25 -> 25, of which waited for: 17 -> 14; matrix products, arithmetic and copies ran while one was open for 0% -> 0% of each run, Pallas kernels for 12% -> 28%
where the time goes in v4:
time: 160 us
  waiting for transfers between devices  51.3 us (32%)
  Pallas kernels  46.5 us (29%)
  blocking collectives  29.4 us (18%)
  starting transfers between devices  23.3 us (15%)
  local copies, waits for them, and re-layouts  5.63 us (4%)
  other arithmetic  2.5 us (2%)
    ppermute x25, waiting for transfers between devices, permute(): return lax.ppermute(array, BOTH, pairs)  51.3 us
    all_to_all x1, blocking collectives, per_device(): lax.all_to_all(packed, BOTH, 0, 0, axis_index_groups=teams, tiled=True)  29.4 us
    pallas_call x3, Pallas kernels, whole_blocks(): pl.pallas_call(functools.partial(whole_kernel, which=which), grid=(steps,...  26.4 us
    ppermute x25, starting transfers between devices, permute(): return lax.ppermute(array, BOTH, pairs)  23.3 us
    pallas_call x1, Pallas kernels, finish(): pl.pallas_call(finish_kernel, grid=(2,), in_specs=[ANY, pl.BlockSpec(tabl...  19 us
  transfers between devices with their start and end apart: 25, of which 14 were waited for; matrix products, arithmetic and copies ran while one was open for 0% of the time, Pallas kernels for 28%

profile of v4, /device:TPU:0, one launch (start us, length us, event | category | flops | bytes accessed | tf_op | source)
XLA Modules:
  0.0 159.7 jit_solution(9655888961047689704)
XLA Ops:
  0.6 1.7 %collective-permute-start = (bf16[160,512]{1,0:T(8,128)(2,1)}, bf16[160,512]{1,0:T(8,128)(2,1)S(1)}, u32[]{:S(2)}, u32[]{:S(2)}) collective-permute-start(bf16[160,512]{1,0:T(8,128)(2,1)} %bitcast.85), channel_id=1, source_target_pairs={{0,8},{1,9},{2,10},{3,11},{4,12},{5,13},{6,14},{7,15},{8,16},{9,17... | collective-permute-start | bytes 491528 | tf_op jit(solution)/shard_map/ppermute | solution.py:39
  2.4 1.6 collective-permute-start.1
  3.9 2.1 %collective-permute-start.2 = (bf16[160,512]{1,0:T(8,128)(2,1)}, bf16[160,512]{1,0:T(8,128)(2,1)S(1)}, u32[]{:S(2)}, u32[]{:S(2)}) collective-permute-start(bf16[160,512]{1,0:T(8,128)(2,1)} %bitcast.87), channel_id=1, source_target_pairs={{0,16},{1,17},{2,18},{3,19},{4,20},{5,21},{6,22},{7,23},{8,24},{9,... | collective-permute-start | bytes 491528 | tf_op jit(solution)/shard_map/ppermute | solution.py:39
  6.0 2.2 %collective-permute-done.lower = bf16[160,512]{1,0:T(8,128)(2,1)S(1)} collective-permute-done((bf16[160,512]{1,0:T(8,128)(2,1)}, bf16[160,512]{1,0:T(8,128)(2,1)S(1)}, u32[]{:S(2)}, u32[]{:S(2)}) %collective-permute-start) | collective-permute-done | bytes 163872 | tf_op jit(solution)/shard_map/ppermute | solution.py:39
  8.2 3.0 %collective-permute-done.1.upper = bf16[160,512]{1,0:T(8,128)(2,1)S(1)} collective-permute-done((bf16[160,512]{1,0:T(8,128)(2,1)}, bf16[160,512]{1,0:T(8,128)(2,1)S(1)}, u32[]{:S(2)}, u32[]{:S(2)}) %collective-permute-start.1) | collective-permute-done | bytes 163872 | tf_op jit(solution)/shard_map/ppermute | solution.py:39
  11.2 1.7 %collective-permute-done.2.far = bf16[160,512]{1,0:T(8,128)(2,1)S(1)} collective-permute-done((bf16[160,512]{1,0:T(8,128)(2,1)}, bf16[160,512]{1,0:T(8,128)(2,1)S(1)}, u32[]{:S(2)}, u32[]{:S(2)}) %collective-permute-start.2) | collective-permute-done | bytes 163872 | tf_op jit(solution)/shard_map/ppermute | solution.py:39
  12.9 0.9 copy-done
  13.8 0.1 shard_map.59
  14.0 1.6 collective-permute-start.3
  15.5 1.9 %collective-permute-start.6 = (bf16[4,160,256]{2,1,0:T(8,128)(2,1)S(1)}, bf16[4,160,256]{2,1,0:T(8,128)(2,1)S(1)}, u32[]{:S(2)}, u32[]{:S(2)}) collective-permute-start(bf16[4,160,256]{2,1,0:T(8,128)(2,1)S(1)} %get-tuple-element.27.refs_4_), channel_id=1, source_target_pairs={{0,1},{1,2},{2,3},{3,0},{4,7},{5,4},{6,5},{7,6},{8,9},{9,10},{10,1... | collective-permute-start | bytes 983048 | tf_op jit(solution)/shard_map/ppermute | solution.py:39
  17.4 1.7 %collective-permute-start.4 = (bf16[4,160,256]{2,1,0:T(8,128)(2,1)S(1)}, bf16[4,160,256]{2,1,0:T(8,128)(2,1)S(1)}, u32[]{:S(2)}, u32[]{:S(2)}) collective-permute-start(bf16[4,160,256]{2,1,0:T(8,128)(2,1)S(1)} %get-tuple-element.26.refs_0_), channel_id=1, source_target_pairs={{0,96},{1,97},{2,98},{3,99},{4,36},{5,37},{6,38},{7,39},{8,104},{9... | collective-permute-start | bytes 983048 | tf_op jit(solution)/shard_map/ppermute | solution.py:39
  19.2 2.1 %collective-permute-start.7 = (bf16[4,160,256]{2,1,0:T(8,128)(2,1)S(1)}, bf16[4,160,256]{2,1,0:T(8,128)(2,1)S(1)}, u32[]{:S(2)}, u32[]{:S(2)}) collective-permute-start(bf16[4,160,256]{2,1,0:T(8,128)(2,1)S(1)} %get-tuple-element.27.refs_4_), channel_id=1, source_target_pairs={{0,3},{1,0},{2,1},{3,2},{4,5},{5,6},{6,7},{7,4},{8,11},{9,8},{10,9... | collective-permute-start | bytes 983048 | tf_op jit(solution)/shard_map/ppermute | solution.py:39
  21.3 1.0 collective-permute-done.3.refs_1_
  22.3 0.7 collective-permute-start.5
  23.0 3.1 %collective-permute-done.6.refs_5_ = bf16[4,160,256]{2,1,0:T(8,128)(2,1)S(1)} collective-permute-done((bf16[4,160,256]{2,1,0:T(8,128)(2,1)S(1)}, bf16[4,160,256]{2,1,0:T(8,128)(2,1)S(1)}, u32[]{:S(2)}, u32[]{:S(2)}) %collective-permute-start.6) | collective-permute-done | bytes 327712 | tf_op jit(solution)/shard_map/ppermute | solution.py:39
  26.1 1.2 collective-permute-start.8
  27.4 3.2 %collective-permute-done.5.refs_3_ = bf16[4,160,256]{2,1,0:T(8,128)(2,1)S(1)} collective-permute-done((bf16[4,160,256]{2,1,0:T(8,128)(2,1)S(1)}, bf16[4,160,256]{2,1,0:T(8,128)(2,1)S(1)}, u32[]{:S(2)}, u32[]{:S(2)}) %collective-permute-start.5) | collective-permute-done | bytes 327712 | tf_op jit(solution)/shard_map/ppermute | solution.py:39
  30.6 4.0 %collective-permute-done.8.refs_7_ = bf16[4,160,256]{2,1,0:T(8,128)(2,1)S(1)} collective-permute-done((bf16[4,160,256]{2,1,0:T(8,128)(2,1)S(1)}, bf16[4,160,256]{2,1,0:T(8,128)(2,1)S(1)}, u32[]{:S(2)}, u32[]{:S(2)}) %collective-permute-start.8) | collective-permute-done | bytes 327712 | tf_op jit(solution)/shard_map/ppermute | solution.py:39
  34.6 0.9 shard_map.60
  35.5 0.1 collective-permute-start.15
  35.6 0.5 collective-permute-start.16
  36.1 2.4 %collective-permute-start.10 = (bf16[4,4,160,256]{3,2,1,0:T(8,128)(2,1)S(1)}, bf16[4,4,160,256]{3,2,1,0:T(8,128)(2,1)S(1)}, u32[]{:S(2)}, u32[]{:S(2)}) collective-permute-start(bf16[4,4,160,256]{3,2,1,0:T(8,128)(2,1)S(1)} %get-tuple-element.29.refs_0_), channel_id=1, source_target_pairs={{0,32},{1,33},{2,34},{3,35},{4,100},{5,101},{6,102},{7,103},{8,40}... | collective-permute-start | bytes 3932168 | tf_op jit(solution)/shard_map/ppermute | solution.py:39
  38.5 0.0 collective-permute-start.9
  38.5 0.4 select_convert_fusion.table_ref
  38.9 0.0 collective-permute-done.15.refs_1_
  38.9 7.8 %shard_map.61 = (f32[16,4,40,128]{3,2,1,0:T(8,128)S(1)}, f32[16,4,40,128]{3,2,1,0:T(8,128)S(1)}) custom-call(bf16[1187,5120]{1,0:T(8,128)(2,1)} %bitcast.89, bf16[512,1187]{1,0:T(8,128)(2,1)S(1)} %select_convert_fusion.table_ref, bf16[4,4,160,256]{3,2,1,0:T(8,128)(2,1)S(1)} %get-tuple-element.28.refs_0_, ...), custom_call_target="tpu_custom_call" | custom-call | flops 3422814208 | bytes 14776320 | tf_op jit(solution)/shard_map/pallas_call | solution.py:205
  46.8 0.0 collective-permute-done.16.refs_1_
  46.8 0.8 collective-permute-start.17
  47.6 7.3 %collective-permute-done.10.refs_2_ = bf16[4,4,160,256]{3,2,1,0:T(8,128)(2,1)S(1)} collective-permute-done((bf16[4,4,160,256]{3,2,1,0:T(8,128)(2,1)S(1)}, bf16[4,4,160,256]{3,2,1,0:T(8,128)(2,1)S(1)}, u32[]{:S(2)}, u32[]{:S(2)}) %collective-permute-start.10) | collective-permute-done | bytes 1310752 | tf_op jit(solution)/shard_map/ppermute | solution.py:39
  54.9 2.4 %collective-permute-done.9.refs_0_ = bf16[4,4,160,256]{3,2,1,0:T(8,128)(2,1)S(1)} collective-permute-done((bf16[4,4,160,256]{3,2,1,0:T(8,128)(2,1)S(1)}, bf16[4,4,160,256]{3,2,1,0:T(8,128)(2,1)S(1)}, u32[]{:S(2)}, u32[]{:S(2)}) %collective-permute-start.9) | collective-permute-done | bytes 1310752 | tf_op jit(solution)/shard_map/ppermute | solution.py:39
  57.3 0.0 collective-permute-start.13
  57.3 0.9 collective-permute-start.19
  58.2 13.2 %collective-permute-done.17.refs_1_ = bf16[4,4,160,256]{3,2,1,0:T(8,128)(2,1)S(1)} collective-permute-done((bf16[4,4,160,256]{3,2,1,0:T(8,128)(2,1)S(1)}, bf16[4,4,160,256]{3,2,1,0:T(8,128)(2,1)S(1)}, u32[]{:S(2)}, u32[]{:S(2)}) %collective-permute-start.17) | collective-permute-done | bytes 1310752 | tf_op jit(solution)/shard_map/ppermute | solution.py:39
  71.4 0.9 collective-permute-start.12
  72.3 0.0 collective-permute-done.13.refs_2_
  72.3 1.7 %collective-permute-start.14 = (bf16[4,4,160,256]{3,2,1,0:T(8,128)(2,1)S(1)}, bf16[4,4,160,256]{3,2,1,0:T(8,128)(2,1)S(1)}, u32[]{:S(2)}, u32[]{:S(2)}) collective-permute-start(bf16[4,4,160,256]{3,2,1,0:T(8,128)(2,1)S(1)} %collective-permute-done.10.refs_2_), channel_id=1, source_target_pairs={{0,4},{1,5},{2,6},{3,7},{4,0},{5,1},{6,2},{7,3},{8,12},{9,13},{10,... | collective-permute-start | bytes 3932168 | tf_op jit(solution)/shard_map/ppermute | solution.py:39
  74.0 2.2 %collective-permute-done.19.refs_3_ = bf16[4,4,160,256]{3,2,1,0:T(8,128)(2,1)S(1)} collective-permute-done((bf16[4,4,160,256]{3,2,1,0:T(8,128)(2,1)S(1)}, bf16[4,4,160,256]{3,2,1,0:T(8,128)(2,1)S(1)}, u32[]{:S(2)}, u32[]{:S(2)}) %collective-permute-start.19) | collective-permute-done | bytes 1310752 | tf_op jit(solution)/shard_map/ppermute | solution.py:39
  76.2 0.0 collective-permute-start.20
  76.2 10.8 %shard_map.62 = (f32[16,4,40,128]{3,2,1,0:T(8,128)S(1)}, f32[16,4,40,128]{3,2,1,0:T(8,128)S(1)}) custom-call(bf16[1187,5120]{1,0:T(8,128)(2,1)} %bitcast.90, bf16[512,1187]{1,0:T(8,128)(2,1)S(1)} %select_convert_fusion.table_ref, bf16[4,4,160,256]{3,2,1,0:T(8,128)(2,1)S(1)} %collective-permute-done.9.refs_0_, ...), custom_call_target="tpu_custom_call", output_to_operand_aliasing={{0}: (6, {}), {1}: (7, {})} | custom-call | flops 6845628416 | bytes 17397760 | tf_op jit(solution)/shard_map/pallas_call | solution.py:205
  86.9 3.3 %collective-permute-done.11.refs_0_ = bf16[4,4,160,256]{3,2,1,0:T(8,128)(2,1)S(1)} collective-permute-done((bf16[4,4,160,256]{3,2,1,0:T(8,128)(2,1)S(1)}, bf16[4,4,160,256]{3,2,1,0:T(8,128)(2,1)S(1)}, u32[]{:S(2)}, u32[]{:S(2)}) %collective-permute-start.11) | collective-permute-done | bytes 1310752 | tf_op jit(solution)/shard_map/ppermute | solution.py:39
  90.2 0.0 collective-permute-done.12.refs_6_
  90.2 1.1 copy-done.5
  91.3 0.5 collective-permute-start.21
  91.9 2.5 %collective-permute-done.23.refs_7_ = bf16[4,4,160,256]{3,2,1,0:T(8,128)(2,1)S(1)} collective-permute-done((bf16[4,4,160,256]{3,2,1,0:T(8,128)(2,1)S(1)}, bf16[4,4,160,256]{3,2,1,0:T(8,128)(2,1)S(1)}, u32[]{:S(2)}, u32[]{:S(2)}) %collective-permute-start.23) | collective-permute-done | bytes 1310752 | tf_op jit(solution)/shard_map/ppermute | solution.py:39
  94.4 1.1 copy-done.6
  95.5 19.0 %shard_map.64 = (f32[16,4,40,128]{3,2,1,0:T(8,128)S(1)}, f32[16,4,40,128]{3,2,1,0:T(8,128)S(1)}) custom-call(bf16[1187,5120]{1,0:T(8,128)(2,1)} %bitcast.91, bf16[512,1187]{1,0:T(8,128)(2,1)S(1)} %select_convert_fusion.table_ref, bf16[4,4,160,256]{3,2,1,0:T(8,128)(2,1)S(1)} %get-tuple-element.29.refs_0_, ...), custom_call_target="tpu_custom_call" | custom-call | flops 13691256832 | bytes 22640640 | tf_op jit(solution)/shard_map/pallas_call | solution.py:301
  114.5 0.4 collective-permute-start.24
  114.9 7.8 %shard_map.63 = (f32[16,4,40,128]{3,2,1,0:T(8,128)S(1)}, f32[16,4,40,128]{3,2,1,0:T(8,128)S(1)}) custom-call(bf16[1187,5120]{1,0:T(8,128)(2,1)} %bitcast.92, bf16[512,1187]{1,0:T(8,128)(2,1)S(1)} %select_convert_fusion.table_ref, bf16[4,4,160,256]{3,2,1,0:T(8,128)(2,1)S(1)} %collective-permute-done.11.refs_0_, ...), custom_call_target="tpu_custom_call", output_to_operand_aliasing={{0}: (4, {}), {1}: (5, {})} | custom-call | flops 3422814208 | bytes 14776320 | tf_op jit(solution)/shard_map/pallas_call | solution.py:205
  122.8 0.5 collective-permute-start.22
  123.6 0.1 fusion.13
  123.7 2.2 %collective-permute-done.22 = f32[16,4,40,128]{3,2,1,0:T(8,128)S(1)} collective-permute-done((f32[16,4,40,128]{3,2,1,0:T(8,128)S(1)}, f32[16,4,40,128]{3,2,1,0:T(8,128)S(1)}, u32[]{:S(2)}, u32[]{:S(2)}) %collective-permute-start.22) | collective-permute-done | bytes 1310752 | tf_op jit(solution)/shard_map/ppermute | solution.py:39
  126.0 0.1 fusion.11
  126.1 0.1 add_convert_fusion
  126.4 0.1 add_convert_fusion.1
  126.7 0.2 fusion.2
  127.0 0.2 fusion.4
  127.2 1.0 concatenate.11
  128.2 29.4 %all_to_all.5 = f16[64,80,128]{2,1,0:T(8,128)(2,1)S(1)} all-to-all(f16[64,80,128]{2,1,0:T(8,128)(2,1)S(1)} %concatenate.11), channel_id=1, replica_groups={{0,1,2,3,8,9,10,11,16,17,18,19,24,25,26,27,32,33,34,35,40,41,42,43,48,4..., dimensions={0} | all-to-all | bytes 2621440 | tf_op jit(solution)/shard_map/all_to_all | solution.py:380
  157.6 0.2 convert.43
  157.9 0.1 fusion.18
  158.0 0.1 fusion.10
  158.1 0.3 fusion
  158.4 0.6 log_negate_fusion
  159.1 0.6 reshape.161
  (49 shorter events, 0.9 us)
Async XLA Ops:
  0.6 7.6 %collective-permute-start = (bf16[160,512]{1,0:T(8,128)(2,1)}, bf16[160,512]{1,0:T(8,128)(2,1)S(1)}, u32[]{:S(2)}, u32[]{:S(2)}) collective-permute-start(bf16[160,512]{1,0:T(8,128)(2,1)} %bitcast.85), channel_id=1, source_target_pairs={{0,8},{1,9},{2,10},{3,11},{4,12},{5,13},{6,14},{7,15},{8,16},{9,17... | collective-permute-start | bytes 491528 | tf_op jit(solution)/shard_map/ppermute | solution.py:39
  2.4 8.8 %collective-permute-start.1 = (bf16[160,512]{1,0:T(8,128)(2,1)}, bf16[160,512]{1,0:T(8,128)(2,1)S(1)}, u32[]{:S(2)}, u32[]{:S(2)}) collective-permute-start(bf16[160,512]{1,0:T(8,128)(2,1)} %bitcast.86), channel_id=1, source_target_pairs={{0,24},{1,25},{2,26},{3,27},{4,28},{5,29},{6,30},{7,31},{8,0},{9,1... | collective-permute-start | bytes 491528 | tf_op jit(solution)/shard_map/ppermute | solution.py:39
  3.9 9.0 %collective-permute-start.2 = (bf16[160,512]{1,0:T(8,128)(2,1)}, bf16[160,512]{1,0:T(8,128)(2,1)S(1)}, u32[]{:S(2)}, u32[]{:S(2)}) collective-permute-start(bf16[160,512]{1,0:T(8,128)(2,1)} %bitcast.87), channel_id=1, source_target_pairs={{0,16},{1,17},{2,18},{3,19},{4,20},{5,21},{6,22},{7,23},{8,24},{9,... | collective-permute-start | bytes 491528 | tf_op jit(solution)/shard_map/ppermute | solution.py:39
  12.9 0.9 copy-start
  14.0 8.4 %collective-permute-start.3 = (bf16[4,160,256]{2,1,0:T(8,128)(2,1)S(1)}, bf16[4,160,256]{2,1,0:T(8,128)(2,1)S(1)}, u32[]{:S(2)}, u32[]{:S(2)}) collective-permute-start(bf16[4,160,256]{2,1,0:T(8,128)(2,1)S(1)} %get-tuple-element.26.refs_0_), channel_id=1, source_target_pairs={{0,32},{1,33},{2,34},{3,35},{4,100},{5,101},{6,102},{7,103},{8,40}... | collective-permute-start | bytes 983048 | tf_op jit(solution)/shard_map/ppermute | solution.py:39
  15.5 20.6 %copy-start.1 = (s32[1187]{0:T(1024)S(1)}, s32[1187]{0:T(1024)}, u32[]{:S(2)}) copy-start(s32[1187]{0:T(1024)} %param.6) | copy-start | bytes 14248
  15.5 23.0 %copy-start.2 = (s32[1187]{0:T(1024)S(1)}, s32[1187]{0:T(1024)}, u32[]{:S(2)}) copy-start(s32[1187]{0:T(1024)} %param.7) | copy-start | bytes 14248
  15.5 10.6 %collective-permute-start.6 = (bf16[4,160,256]{2,1,0:T(8,128)(2,1)S(1)}, bf16[4,160,256]{2,1,0:T(8,128)(2,1)S(1)}, u32[]{:S(2)}, u32[]{:S(2)}) collective-permute-start(bf16[4,160,256]{2,1,0:T(8,128)(2,1)S(1)} %get-tuple-element.27.refs_4_), channel_id=1, source_target_pairs={{0,1},{1,2},{2,3},{3,0},{4,7},{5,4},{6,5},{7,6},{8,9},{9,10},{10,1... | collective-permute-start | bytes 983048 | tf_op jit(solution)/shard_map/ppermute | solution.py:39
  17.4 9.9 %collective-permute-start.4 = (bf16[4,160,256]{2,1,0:T(8,128)(2,1)S(1)}, bf16[4,160,256]{2,1,0:T(8,128)(2,1)S(1)}, u32[]{:S(2)}, u32[]{:S(2)}) collective-permute-start(bf16[4,160,256]{2,1,0:T(8,128)(2,1)S(1)} %get-tuple-element.26.refs_0_), channel_id=1, source_target_pairs={{0,96},{1,97},{2,98},{3,99},{4,36},{5,37},{6,38},{7,39},{8,104},{9... | collective-permute-start | bytes 983048 | tf_op jit(solution)/shard_map/ppermute | solution.py:39
  19.2 8.2 %collective-permute-start.7 = (bf16[4,160,256]{2,1,0:T(8,128)(2,1)S(1)}, bf16[4,160,256]{2,1,0:T(8,128)(2,1)S(1)}, u32[]{:S(2)}, u32[]{:S(2)}) collective-permute-start(bf16[4,160,256]{2,1,0:T(8,128)(2,1)S(1)} %get-tuple-element.27.refs_4_), channel_id=1, source_target_pairs={{0,3},{1,0},{2,1},{3,2},{4,5},{5,6},{6,7},{7,4},{8,11},{9,8},{10,9... | collective-permute-start | bytes 983048 | tf_op jit(solution)/shard_map/ppermute | solution.py:39
  22.3 8.3 %collective-permute-start.5 = (bf16[4,160,256]{2,1,0:T(8,128)(2,1)S(1)}, bf16[4,160,256]{2,1,0:T(8,128)(2,1)S(1)}, u32[]{:S(2)}, u32[]{:S(2)}) collective-permute-start(bf16[4,160,256]{2,1,0:T(8,128)(2,1)S(1)} %collective-permute-done.3.refs_1_), channel_id=1, source_target_pairs={{0,32},{1,33},{2,34},{3,35},{4,100},{5,101},{6,102},{7,103},{8,40}... | collective-permute-start | bytes 983048 | tf_op jit(solution)/shard_map/ppermute | solution.py:39
  26.1 8.5 %collective-permute-start.8 = (bf16[4,160,256]{2,1,0:T(8,128)(2,1)S(1)}, bf16[4,160,256]{2,1,0:T(8,128)(2,1)S(1)}, u32[]{:S(2)}, u32[]{:S(2)}) collective-permute-start(bf16[4,160,256]{2,1,0:T(8,128)(2,1)S(1)} %collective-permute-done.6.refs_5_), channel_id=1, source_target_pairs={{0,1},{1,2},{2,3},{3,0},{4,7},{5,4},{6,5},{7,6},{8,9},{9,10},{10,1... | collective-permute-start | bytes 983048 | tf_op jit(solution)/shard_map/ppermute | solution.py:39
  35.5 3.4 %collective-permute-start.15 = (bf16[4,4,160,256]{3,2,1,0:T(8,128)(2,1)S(1)}, bf16[4,4,160,256]{3,2,1,0:T(8,128)(2,1)S(1)}, u32[]{:S(2)}, u32[]{:S(2)}) collective-permute-start(bf16[4,4,160,256]{3,2,1,0:T(8,128)(2,1)S(1)} %get-tuple-element.28.refs_0_), channel_id=1, source_target_pairs={{0,4},{1,5},{2,6},{3,7},{4,0},{5,1},{6,2},{7,3},{8,12},{9,13},{10,... | collective-permute-start | bytes 3932168 | tf_op jit(solution)/shard_map/ppermute | solution.py:39
  35.6 11.2 %collective-permute-start.16 = (bf16[4,4,160,256]{3,2,1,0:T(8,128)(2,1)S(1)}, bf16[4,4,160,256]{3,2,1,0:T(8,128)(2,1)S(1)}, u32[]{:S(2)}, u32[]{:S(2)}) collective-permute-start(bf16[4,4,160,256]{3,2,1,0:T(8,128)(2,1)S(1)} %get-tuple-element.29.refs_0_), channel_id=1, source_target_pairs={{0,4},{1,5},{2,6},{3,7},{4,0},{5,1},{6,2},{7,3},{8,12},{9,13},{10,... | collective-permute-start | bytes 3932168 | tf_op jit(solution)/shard_map/ppermute | solution.py:39
  36.1 18.8 %collective-permute-start.10 = (bf16[4,4,160,256]{3,2,1,0:T(8,128)(2,1)S(1)}, bf16[4,4,160,256]{3,2,1,0:T(8,128)(2,1)S(1)}, u32[]{:S(2)}, u32[]{:S(2)}) collective-permute-start(bf16[4,4,160,256]{3,2,1,0:T(8,128)(2,1)S(1)} %get-tuple-element.29.refs_0_), channel_id=1, source_target_pairs={{0,32},{1,33},{2,34},{3,35},{4,100},{5,101},{6,102},{7,103},{8,40}... | collective-permute-start | bytes 3932168 | tf_op jit(solution)/shard_map/ppermute | solution.py:39
  38.5 18.8 %collective-permute-start.9 = (bf16[4,4,160,256]{3,2,1,0:T(8,128)(2,1)S(1)}, bf16[4,4,160,256]{3,2,1,0:T(8,128)(2,1)S(1)}, u32[]{:S(2)}, u32[]{:S(2)}) collective-permute-start(bf16[4,4,160,256]{3,2,1,0:T(8,128)(2,1)S(1)} %get-tuple-element.28.refs_0_), channel_id=1, source_target_pairs={{0,1},{1,2},{2,3},{3,0},{4,7},{5,4},{6,5},{7,6},{8,9},{9,10},{10,1... | collective-permute-start | bytes 3932168 | tf_op jit(solution)/shard_map/ppermute | solution.py:39
  46.8 24.6 %collective-permute-start.17 = (bf16[4,4,160,256]{3,2,1,0:T(8,128)(2,1)S(1)}, bf16[4,4,160,256]{3,2,1,0:T(8,128)(2,1)S(1)}, u32[]{:S(2)}, u32[]{:S(2)}) collective-permute-start(bf16[4,4,160,256]{3,2,1,0:T(8,128)(2,1)S(1)} %collective-permute-done.15.refs_1_), channel_id=1, source_target_pairs={{0,1},{1,2},{2,3},{3,0},{4,7},{5,4},{6,5},{7,6},{8,9},{9,10},{10,1... | collective-permute-start | bytes 3932168 | tf_op jit(solution)/shard_map/ppermute | solution.py:39
  57.3 14.9 %collective-permute-start.13 = (bf16[4,4,160,256]{3,2,1,0:T(8,128)(2,1)S(1)}, bf16[4,4,160,256]{3,2,1,0:T(8,128)(2,1)S(1)}, u32[]{:S(2)}, u32[]{:S(2)}) collective-permute-start(bf16[4,4,160,256]{3,2,1,0:T(8,128)(2,1)S(1)} %collective-permute-done.9.refs_0_), channel_id=1, source_target_pairs={{0,4},{1,5},{2,6},{3,7},{4,0},{5,1},{6,2},{7,3},{8,12},{9,13},{10,... | collective-permute-start | bytes 3932168 | tf_op jit(solution)/shard_map/ppermute | solution.py:39
  57.3 18.8 %collective-permute-start.19 = (bf16[4,4,160,256]{3,2,1,0:T(8,128)(2,1)S(1)}, bf16[4,4,160,256]{3,2,1,0:T(8,128)(2,1)S(1)}, u32[]{:S(2)}, u32[]{:S(2)}) collective-permute-start(bf16[4,4,160,256]{3,2,1,0:T(8,128)(2,1)S(1)} %collective-permute-done.16.refs_1_), channel_id=1, source_target_pairs={{0,32},{1,33},{2,34},{3,35},{4,100},{5,101},{6,102},{7,103},{8,40}... | collective-permute-start | bytes 3932168 | tf_op jit(solution)/shard_map/ppermute | solution.py:39
  71.4 4.8 %collective-permute-start.18 = (bf16[4,4,160,256]{3,2,1,0:T(8,128)(2,1)S(1)}, bf16[4,4,160,256]{3,2,1,0:T(8,128)(2,1)S(1)}, u32[]{:S(2)}, u32[]{:S(2)}) collective-permute-start(bf16[4,4,160,256]{3,2,1,0:T(8,128)(2,1)S(1)} %collective-permute-done.17.refs_1_), channel_id=1, source_target_pairs={{0,4},{1,5},{2,6},{3,7},{4,0},{5,1},{6,2},{7,3},{8,12},{9,13},{10,... | collective-permute-start | bytes 3932168 | tf_op jit(solution)/shard_map/ppermute | solution.py:39
  71.4 18.8 %collective-permute-start.11 = (bf16[4,4,160,256]{3,2,1,0:T(8,128)(2,1)S(1)}, bf16[4,4,160,256]{3,2,1,0:T(8,128)(2,1)S(1)}, u32[]{:S(2)}, u32[]{:S(2)}) collective-permute-start(bf16[4,4,160,256]{3,2,1,0:T(8,128)(2,1)S(1)} %collective-permute-done.9.refs_0_), channel_id=1, source_target_pairs={{0,1},{1,2},{2,3},{3,0},{4,7},{5,4},{6,5},{7,6},{8,9},{9,10},{10,1... | collective-permute-start | bytes 3932168 | tf_op jit(solution)/shard_map/ppermute | solution.py:39
  71.4 18.8 %collective-permute-start.12 = (bf16[4,4,160,256]{3,2,1,0:T(8,128)(2,1)S(1)}, bf16[4,4,160,256]{3,2,1,0:T(8,128)(2,1)S(1)}, u32[]{:S(2)}, u32[]{:S(2)}) collective-permute-start(bf16[4,4,160,256]{3,2,1,0:T(8,128)(2,1)S(1)} %collective-permute-done.10.refs_2_), channel_id=1, source_target_pairs={{0,32},{1,33},{2,34},{3,35},{4,100},{5,101},{6,102},{7,103},{8,40}... | collective-permute-start | bytes 3932168 | tf_op jit(solution)/shard_map/ppermute | solution.py:39
  72.3 18.0 %collective-permute-start.14 = (bf16[4,4,160,256]{3,2,1,0:T(8,128)(2,1)S(1)}, bf16[4,4,160,256]{3,2,1,0:T(8,128)(2,1)S(1)}, u32[]{:S(2)}, u32[]{:S(2)}) collective-permute-start(bf16[4,4,160,256]{3,2,1,0:T(8,128)(2,1)S(1)} %collective-permute-done.10.refs_2_), channel_id=1, source_target_pairs={{0,4},{1,5},{2,6},{3,7},{4,0},{5,1},{6,2},{7,3},{8,12},{9,13},{10,... | collective-permute-start | bytes 3932168 | tf_op jit(solution)/shard_map/ppermute | solution.py:39
  76.2 14.1 %collective-permute-start.20 = (bf16[4,4,160,256]{3,2,1,0:T(8,128)(2,1)S(1)}, bf16[4,4,160,256]{3,2,1,0:T(8,128)(2,1)S(1)}, u32[]{:S(2)}, u32[]{:S(2)}) collective-permute-start(bf16[4,4,160,256]{3,2,1,0:T(8,128)(2,1)S(1)} %collective-permute-done.19.refs_3_), channel_id=1, source_target_pairs={{0,4},{1,5},{2,6},{3,7},{4,0},{5,1},{6,2},{7,3},{8,12},{9,13},{10,... | collective-permute-start | bytes 3932168 | tf_op jit(solution)/shard_map/ppermute | solution.py:39
  90.2 4.2 %copy-start.3 = (bf16[4,4,160,256]{3,2,1,0:T(8,128)(2,1)}, bf16[4,4,160,256]{3,2,1,0:T(8,128)(2,1)S(1)}, u32[]{:S(2)}) copy-start(bf16[4,4,160,256]{3,2,1,0:T(8,128)(2,1)S(1)} %collective-permute-done.12.refs_6_) | copy-start | bytes 3932164
  90.2 4.2 %copy-start.4 = (bf16[4,4,160,256]{3,2,1,0:T(8,128)(2,1)}, bf16[4,4,160,256]{3,2,1,0:T(8,128)(2,1)S(1)}, u32[]{:S(2)}) copy-start(bf16[4,4,160,256]{3,2,1,0:T(8,128)(2,1)S(1)} %collective-permute-done.14.refs_4_) | copy-start | bytes 3932164
  90.2 1.1 copy-start.5
  91.3 3.0 %collective-permute-start.23 = (bf16[4,4,160,256]{3,2,1,0:T(8,128)(2,1)S(1)}, bf16[4,4,160,256]{3,2,1,0:T(8,128)(2,1)S(1)}, u32[]{:S(2)}, u32[]{:S(2)}) collective-permute-start(bf16[4,4,160,256]{3,2,1,0:T(8,128)(2,1)S(1)} %collective-permute-done.12.refs_6_), channel_id=1, source_target_pairs={{0,4},{1,5},{2,6},{3,7},{4,0},{5,1},{6,2},{7,3},{8,12},{9,13},{10,... | collective-permute-start | bytes 3932168 | tf_op jit(solution)/shard_map/ppermute | solution.py:39
  91.3 23.6 %collective-permute-start.21 = (bf16[4,4,160,256]{3,2,1,0:T(8,128)(2,1)S(1)}, bf16[4,4,160,256]{3,2,1,0:T(8,128)(2,1)S(1)}, u32[]{:S(2)}, u32[]{:S(2)}) collective-permute-start(bf16[4,4,160,256]{3,2,1,0:T(8,128)(2,1)S(1)} %collective-permute-done.11.refs_0_), channel_id=1, source_target_pairs={{0,4},{1,5},{2,6},{3,7},{4,0},{5,1},{6,2},{7,3},{8,12},{9,13},{10,... | collective-permute-start | bytes 3932168 | tf_op jit(solution)/shard_map/ppermute | solution.py:39
  94.4 1.1 copy-start.6
  114.5 9.0 %collective-permute-start.24 = (f32[16,4,40,128]{3,2,1,0:T(8,128)S(1)}, f32[16,4,40,128]{3,2,1,0:T(8,128)S(1)}, u32[]{:S(2)}, u32[]{:S(2)}) collective-permute-start(f32[16,4,40,128]{3,2,1,0:T(8,128)S(1)} %get-tuple-element.49), channel_id=1, source_target_pairs={{0,4},{1,5},{2,6},{3,7},{4,0},{5,1},{6,2},{7,3},{8,12},{9,13},{10,... | collective-permute-start | bytes 3932168 | tf_op jit(solution)/shard_map/ppermute | solution.py:39
  122.8 3.1 %collective-permute-start.22 = (f32[16,4,40,128]{3,2,1,0:T(8,128)S(1)}, f32[16,4,40,128]{3,2,1,0:T(8,128)S(1)}, u32[]{:S(2)}, u32[]{:S(2)}) collective-permute-start(f32[16,4,40,128]{3,2,1,0:T(8,128)S(1)} %get-tuple-element.44), channel_id=1, source_target_pairs={{0,4},{1,5},{2,6},{3,7},{4,0},{5,1},{6,2},{7,3},{8,12},{9,13},{10,... | collective-permute-start | bytes 3932168 | tf_op jit(solution)/shard_map/ppermute | solution.py:39
